TPU v7x, 512 devices: a whole 4x8x8 slice. The times are simulated.
512 devices in a mesh: seq: 64 (over y, z), head: 8 (over x, core).
Axes of the slice: x: 4, y: 8, z: 8, core: 2. Of those that a mesh axis runs over, the one named last changes fastest.
Arguments:
- byte_stream: bfloat16 [8192, 2048], P('seq', 'head'), may hold values from -6 to 6
- gate_stream: bfloat16 [8192, 2048], P('seq', 'head'), may hold values from -6 to 6
- conv_weight: float32 [4, 2048], P(None, 'head'), may hold values from -3 to 3
- state_write: bfloat16 [8192, 128], P('seq'), may hold values from -6 to 6
- state_read: bfloat16 [8192, 128], P('seq'), may hold values from -0.5 to 0.5
- step_size: float32 [8192, 32], P('seq', 'head'), as said below
- decay_coef: float32 [32], P('head'), as said below
- skip_gain: float32 [32], P('head'), may hold values from 0.5 to 2
- norm_gain: float32 [2048], P('head'), may hold values from 0.25 to 1.75
- mixer_out: bfloat16 [2048, 1024], P('head'), may hold values from -0.125 to 0.125
- residual: bfloat16 [8192, 1024], P('seq'), may hold values from -6 to 6
- boundaries: int32 [64, 32], P('seq'), may hold values from 0 to 8192, as said below
- span_counts: int32 [64], P('seq'), may hold values from 8 to 32, as said below
- span_offsets: int32 [64], P('seq'), may hold values from 0 to 1016, as said below
- pad_vector: bfloat16 [3072], replicated, may hold values from -6 to 6
- main_gain: float32 [4096], replicated, may hold values from 0.25 to 1.75
- query_weight: bfloat16 [4096, 4096], P('seq', 'head')
- key_value_weight: bfloat16 [4096, 2048], P('seq', 'head')
- main_out_weight: bfloat16 [4096, 1024], P('head'), may hold values from -0.09375 to 0.09375
Outputs:
- byte_output: bfloat16 [8192, 1024], P('seq', 'head')
Inputs may be any that keep to these rules, and one draw needn't show every extreme that they name: `boundaries`: row b lists span_counts[b] increasing byte positions of bytes b * 128 to (b + 1) * 128 - 1, the first being b * 128; the other entries are 8192. `span_counts`: they sum to 1024; one block holds exactly 32. `span_offsets`: the exclusive prefix sums of span_counts. `step_size`: Positive. `decay_coef`: Positive.
All inputs are finite; a program needn't handle non-finite values.
Results may differ from a plain program's by a relative error of at most 0.03.
Values may be sent and summed in bfloat16 or wider, within the bound.
A program may use at most 64 MiB of HBM per device.

v0:
```python
import math

import jax
import jax.numpy as jnp
from jax import lax
from jax.sharding import PartitionSpec as P

NH = 32
HP = 64
NGROUP = 8
HD = 128


THETA = 500000.0
EPSILON = 1e-05
PRECISE = lax.Precision.HIGHEST
FARAWAY = 1073741824


def from_behind(block, axis, distance):
    devices = range(lax.axis_size(axis))
    route = [(i - distance, i) for i in devices if i - distance in devices]
    return lax.ppermute(block, axis, route)


def carried_in(value, axis, join, neutral):
    count, mine = (lax.axis_size(axis), lax.axis_index(axis))
    pieces = jax.tree.map(lambda part: lax.all_gather(part, axis), value)
    so_far = jax.tree.map(
        lambda part, zero: jnp.full_like(part, 0) + jnp.asarray(zero, part.dtype), value, neutral
    )

    def step(position, so_far):
        longer = join(so_far, jax.tree.map(lambda part: part[position], pieces))
        return jax.tree.map(lambda new, old: jnp.where(position < mine, new, old), longer, so_far)

    return lax.fori_loop(0, count - 1, step, so_far)


def convolve(inputs, conv_weight, front_rows):
    tap_count = conv_weight.shape[0]
    extended = jnp.concatenate([front_rows, inputs], axis=0).astype(jnp.float32)
    summed = jnp.zeros(inputs.shape, jnp.float32)
    for tap_index in range(tap_count):
        summed = (
            summed
            + conv_weight[tap_index][None, :] * extended[tap_index : tap_index + inputs.shape[0]]
        )
    return jax.nn.silu(summed).astype(jnp.bfloat16)


def scan_block(carried_state, x_block, write_block, read_block, log_decay, input_gain):
    block_size = x_block.shape[0]
    running = jnp.cumsum(log_decay, axis=0)
    affinity = jnp.dot(read_block, write_block.T, preferred_element_type=jnp.float32)
    causal = jnp.arange(block_size)[:, None] >= jnp.arange(block_size)[None, :]
    across = running.T
    spread = jnp.where(causal[None], across[:, :, None] - across[:, None, :], 0.0)
    mixing = (
        jnp.where(causal[None], jnp.exp(spread), 0.0) * affinity[None] * input_gain.T[:, None, :]
    )
    mixing = mixing.astype(jnp.bfloat16)
    within = jnp.einsum("hts,shp->thp", mixing, x_block, preferred_element_type=jnp.float32)
    entering = (
        jnp.einsum("tn,hpn->thp", read_block.astype(jnp.float32), carried_state, precision=PRECISE)
        * jnp.exp(running)[:, :, None]
    )
    remaining = jnp.exp(running[-1][None, :] - running) * input_gain
    updated = jnp.exp(running[-1])[:, None, None] * carried_state + jnp.einsum(
        "sh,shp,sn->hpn",
        remaining,
        x_block.astype(jnp.float32),
        write_block.astype(jnp.float32),
        precision=PRECISE,
    )
    return (updated, within + entering)


def rotate(vectors, positions):
    half_size = vectors.shape[-1] // 2
    frequency = jnp.exp(
        jnp.arange(half_size, dtype=jnp.float32) * (-2.0 * math.log(THETA) / vectors.shape[-1])
    )
    angles = positions.astype(jnp.float32)[:, None] * frequency[None, :]
    cosine = jnp.cos(angles)[:, None, :]
    sine_part = jnp.sin(angles)[:, None, :]
    leading = vectors[..., :half_size]
    trailing = vectors[..., half_size:]
    return jnp.concatenate(
        [leading * cosine - trailing * sine_part, trailing * cosine + leading * sine_part], axis=-1
    )


def combine_states(earlier, after_part):
    return (
        earlier[0] + after_part[0],
        jnp.exp(after_part[0])[:, None, None] * earlier[1] + after_part[1],
    )


def shards(
    byte_stream,
    gate_stream,
    conv_weight,
    state_write,
    state_read,
    step_size,
    decay_coef,
    skip_gain,
    norm_gain,
    mixer_out,
    residual,
    boundaries,
    span_counts,
    span_offsets,
    pad_vector,
    main_gain,
    query_weight,
    key_value_weight,
    main_out_weight,
):
    length = byte_stream.shape[0]
    head_count = step_size.shape[1]
    head_size = byte_stream.shape[1] // head_count
    tap_count = conv_weight.shape[0]
    front_rows = from_behind(byte_stream[length - tap_count + 1 :], "seq", 1)
    conv_out = convolve(byte_stream, conv_weight, front_rows)
    log_decay = -step_size * decay_coef[None, :]
    input_gain = jnp.sqrt(-jnp.expm1(2.0 * log_decay))
    x_heads = conv_out.reshape(length, head_count, head_size)
    carried_state = jnp.zeros((head_count, head_size, state_write.shape[1]), jnp.float32)
    carried_state, block_out = scan_block(
        carried_state, x_heads, state_write, state_read, log_decay, input_gain
    )
    mixed = block_out
    device_running = jnp.cumsum(log_decay, axis=0)
    identity = (jnp.zeros((head_count,), jnp.float32), jnp.zeros_like(carried_state))
    incoming = carried_in((device_running[-1], carried_state), "seq", combine_states, identity)[1]
    mixed = (
        mixed
        + jnp.einsum("tn,hpn->thp", state_read.astype(jnp.float32), incoming, precision=PRECISE)
        * jnp.exp(device_running)[:, :, None]
    )
    mixed = mixed + skip_gain[None, :, None] * x_heads.astype(jnp.float32)
    gated = mixed.reshape(length, -1) * jax.nn.silu(gate_stream.astype(jnp.float32))
    group_width = NH * HP // NGROUP
    shaped = gated.reshape(length, -1, group_width)
    scaled = shaped * lax.rsqrt(jnp.mean(shaped * shaped, axis=-1, keepdims=True) + EPSILON)
    normed = (scaled.reshape(length, -1) * norm_gain[None, :]).astype(jnp.bfloat16)
    partial_enc = jnp.dot(normed, mixer_out, preferred_element_type=jnp.float32)
    capacity = boundaries.shape[1]
    seq_where = lax.axis_index("seq")
    seq_count = lax.axis_size("seq")
    head_where = lax.axis_index("head")
    feature_share = residual.shape[1] // lax.axis_size("head")
    slot_index = jnp.arange(capacity, dtype=jnp.int32)
    usable = slot_index < span_counts[0]
    local_place = boundaries[0] - seq_where * length
    byte_place = jnp.arange(length, dtype=jnp.int32)
    picker = ((local_place[:, None] == byte_place[None, :]) & usable[:, None]).astype(jnp.bfloat16)
    encoded = (
        residual.astype(jnp.float32)
        + lax.psum(partial_enc.astype(jnp.bfloat16), "head").astype(jnp.float32)
    ).astype(jnp.bfloat16)
    span_in = jnp.dot(picker, encoded, preferred_element_type=jnp.float32).astype(jnp.bfloat16)
    encoded_share = lax.dynamic_slice_in_dim(encoded, head_where * feature_share, feature_share, 1)
    table_offsets, table_counts = (
        lax.all_gather(span_offsets, "seq", axis=0, tiled=True),
        lax.all_gather(span_counts, "seq", axis=0, tiled=True),
    )
    query_place = jnp.where(usable, span_offsets[0] + slot_index, FARAWAY - 1)
    rotary_place = jnp.where(usable, span_offsets[0] + slot_index, 0)

    def key_place(gathered_rows):
        owner = gathered_rows // capacity
        inside = gathered_rows % capacity
        matches = owner[:, None] == jnp.arange(seq_count, dtype=jnp.int32)[None, :]
        owner_count = jnp.sum(jnp.where(matches, table_counts[None, :], 0), axis=1)
        owner_offset = jnp.sum(jnp.where(matches, table_offsets[None, :], 0), axis=1)
        return jnp.where(inside < owner_count, owner_offset + inside, FARAWAY)

    row_count = span_in.shape[0]
    lifted = jnp.concatenate(
        [
            span_in.astype(jnp.float32),
            jnp.broadcast_to(
                pad_vector.astype(jnp.float32)[None, :], (row_count, pad_vector.shape[0])
            ),
        ],
        axis=1,
    )
    main_normed = (
        lifted
        * lax.rsqrt(jnp.mean(lifted * lifted, axis=1, keepdims=True) + EPSILON)
        * main_gain[None, :]
    ).astype(jnp.bfloat16)
    query_all = jnp.dot(
        main_normed,
        lax.all_gather(query_weight, "seq", axis=0, tiled=True),
        preferred_element_type=jnp.float32,
    )
    pair_all = jnp.dot(
        main_normed,
        lax.all_gather(key_value_weight, "seq", axis=0, tiled=True),
        preferred_element_type=jnp.float32,
    )
    query_heads = query_weight.shape[1] // HD
    key_heads = key_value_weight.shape[1] // (2 * HD)
    group_size = query_heads // key_heads
    query_vectors = (
        rotate(query_all.reshape(row_count, query_heads, HD), rotary_place)
        .astype(jnp.bfloat16)
        .reshape(row_count, key_heads, group_size, HD)
    )
    pairs = pair_all.reshape(row_count, key_heads, 2, HD)
    keys = (
        rotate(pairs[:, :, 0], rotary_place).astype(jnp.bfloat16).reshape(row_count, key_heads * HD)
    )
    values = pairs[:, :, 1].astype(jnp.bfloat16).reshape(row_count, key_heads * HD)
    start_carry = (
        jnp.full((key_heads, group_size, row_count), -1e30, jnp.float32),
        jnp.zeros((key_heads, group_size, row_count), jnp.float32),
        jnp.zeros((key_heads, group_size, row_count, HD), jnp.float32),
    )
    key_rows = lax.all_gather(keys, "seq", axis=0, tiled=True)
    value_rows = lax.all_gather(values, "seq", axis=0, tiled=True)
    key_count = key_rows.shape[0]
    key_step = math.gcd(key_count, 1024)

    def one_block(running_carry, turn_index):
        highest, total, weighted = running_carry
        key_tile_rows = lax.dynamic_slice_in_dim(
            key_rows, turn_index * key_step, key_step, 0
        ).reshape(key_step, key_heads, HD)
        value_block = lax.dynamic_slice_in_dim(
            value_rows, turn_index * key_step, key_step, 0
        ).reshape(key_step, key_heads, HD)
        placed = key_place(turn_index * key_step + jnp.arange(key_step, dtype=jnp.int32))
        scores = jnp.einsum(
            "afpe,rfe->fpar", query_vectors, key_tile_rows, preferred_element_type=jnp.float32
        ) / math.sqrt(HD)
        allowed = placed[None, None, None, :] <= query_place[None, None, :, None]
        new_highest = jnp.maximum(highest, jnp.max(jnp.where(allowed, scores, -1e30), axis=-1))
        weights = jnp.where(allowed, jnp.exp(scores - new_highest[..., None]), 0.0)
        shrink = jnp.exp(highest - new_highest)
        total = total * shrink + jnp.sum(weights, axis=-1)
        weighted = weighted * shrink[..., None] + jnp.einsum(
            "pszj,jpl->pszl",
            weights.astype(jnp.bfloat16),
            value_block,
            preferred_element_type=jnp.float32,
        )
        return ((new_highest, total, weighted), None)

    result, unused = lax.scan(one_block, start_carry, jnp.arange(key_count // key_step))
    highest, total, weighted = result
    attended = (
        (weighted / total[..., None])
        .astype(jnp.bfloat16)
        .transpose(2, 0, 1, 3)
        .reshape(row_count, -1)
    )
    partial_main = jnp.dot(attended, main_out_weight, preferred_element_type=jnp.float32)
    summed = lax.psum_scatter(
        partial_main.astype(jnp.bfloat16), "head", scatter_dimension=1, tiled=True
    ).astype(jnp.float32)
    rows_share_in = lax.dynamic_slice_in_dim(span_in, head_where * feature_share, feature_share, 1)
    main_rows = (rows_share_in.astype(jnp.float32) + summed).astype(jnp.bfloat16)
    before = (
        jnp.sum(
            ((local_place[None, :] <= byte_place[:, None]) & usable[None, :]).astype(jnp.int32),
            axis=1,
        )
        - 1
    )
    spreader = (before[:, None] == slot_index[None, :]).astype(jnp.bfloat16)
    return (
        encoded_share.astype(jnp.float32)
        + jnp.dot(spreader, main_rows, preferred_element_type=jnp.float32)
    ).astype(jnp.bfloat16)


def solution(mesh):
    in_specs = (
        P("seq", "head"),
        P("seq", "head"),
        P(None, "head"),
        P("seq", None),
        P("seq", None),
        P("seq", "head"),
        P("head"),
        P("head"),
        P("head"),
        P("head", None),
        P("seq", None),
        P("seq", None),
        P("seq"),
        P("seq"),
        P(),
        P(),
        P("seq", "head"),
        P("seq", "head"),
        P("head", None),
    )
    out_specs = P("seq", "head")
    return jax.shard_map(shards, mesh=mesh, in_specs=in_specs, out_specs=out_specs, check_vma=False)
```

profile of v0, /device:TPU:1, one launch (start us, length us, event | category | flops | bytes accessed | tf_op | source)
XLA Modules:
  0.0 578.8 jit_solution(13574909980031613279)
XLA Ops:
  7.5 4.8 collective-permute-start
  16.0 1.6 convolution_add_fusion
  18.0 39.0 %all-gather.2 = f32[64,1,4]{2,1,0:T(1,128)S(1)} all-gather(f32[1,1,4]{2,1,0:T(1,128)S(1)} %get-tuple-element.355), channel_id=1, replica_groups=mesh['seq'=64,'head'=8] {'seq'}, dimensions={0}, use_global_device_ids=true | all-gather | bytes 1040 | tf_op jit(solution)/shard_map/all_gather | solution.py:28
  59.0 62.9 %all-gather.11.cloned.1.call-done = f32[256,64,128]{2,1,0:T(8,128)} async-done(((f32[4,64,128]{2,1,0:T(8,128)}), f32[256,64,128]{2,1,0:T(8,128)}) %all-gather.11.cloned.1.call-update) | async-done | bytes 8388624 | tf_op jit(solution)/shard_map/all_gather | solution.py:28
  121.8 65.2 %while.31 = (s32[]{:T(128)}, f32[4,64,128]{2,1,0:T(8,128)S(1)}, s32[]{:T(128)}, f32[64,4]{1,0:T(8,128)S(1)}, f32[64,4,64,128]{3,2,1,0:T(8,128)}, /*index=5*/s32[]{:T(128)}, s32[]{:T(128)}) while((s32[]{:T(128)}, f32[4,64,128]{2,1,0:T(8,128)S(1)}, s32[]{:T(128)}, f32[64,4]{1,0:T(8,128)S(1)}, f32[64,4,64,128]{3,2,1,0:T(8,128)}, ...), condition=%wide.region_2.3_spmd.clone, body=%wide.region_1.2_spmd.clone.sunk | while | flops 131076 | bytes 393369 | solution.py:37
  121.9 1.0 fusion.110
  123.9 1.0 fusion.110
  125.0 1.0 fusion.110
  126.0 1.0 fusion.110
  127.0 1.0 fusion.110
  191.6 1.3 dynamic-slice
  194.4 18.3 %all-reduce.2 = (s32[64]{0:T(128)S(1)}, s32[64]{0:T(128)S(1)}) all-reduce(s32[64]{0:T(128)S(1)} %dynamic-update-slice, s32[64]{0:T(128)S(1)} %dynamic-update-slice.1), channel_id=1, replica_groups=mesh['seq'=64,'head'=8] {'seq'}, use_global_device_ids=true, to_apply=%add | all-reduce | flops 128 | bytes 1024
  213.1 43.3 %all-reduce.5.cloned.1.call-done = bf16[128,1024]{1,0:T(8,128)(2,1)} async-done(((bf16[128,1024]{1,0:T(8,128)(2,1)}), bf16[128,1024]{1,0:T(8,128)(2,1)}) %all-reduce.5.cloned.1.call-update) | async-done | bytes 262160 | tf_op jit(solution)/shard_map/psum | solution.py:163
  256.4 1.0 add_convert_fusion
  257.8 82.5 %all-gather.7.cloned.1.call-done = bf16[4096,256]{1,0:T(8,128)(2,1)} async-done(((bf16[64,256]{1,0:T(8,128)(2,1)}), bf16[4096,256]{1,0:T(8,128)(2,1)}) %all-gather.7.cloned.1.call-update) | async-done | bytes 2097168 | tf_op jit(solution)/shard_map/all_gather | solution.py:204
  340.3 2.1 fusion.56
  342.5 85.1 %all-gather.9.cloned.1.call-done = bf16[4096,512]{1,0:T(8,128)(2,1)} async-done(((bf16[64,512]{1,0:T(8,128)(2,1)}), bf16[4096,512]{1,0:T(8,128)(2,1)}) %all-gather.9.cloned.1.call-update) | async-done | bytes 4194320 | tf_op jit(solution)/shard_map/all_gather | solution.py:199
  427.6 3.0 fusion.54
  431.0 36.1 %all_gather.33 = bf16[2048,128]{1,0:T(8,128)(2,1)S(1)} all-gather(bf16[32,128]{1,0:T(8,128)(2,1)S(1)} %pad_maximum_fusion.2), channel_id=1, replica_groups=mesh['seq'=64,'head'=8] {'seq'}, dimensions={0}, use_global_device_ids=true | all-gather | bytes 532480 | tf_op jit(solution)/shard_map/all_gather | solution.py:225
  467.1 36.1 %all-gather.1 = bf16[2048,1,1,128]{3,0,2,1:T(8,128)(2,1)S(1)} all-gather(bf16[32,1,1,128]{3,0,2,1:T(8,128)(2,1)S(1)} %copy.96), channel_id=3, replica_groups=mesh['seq'=64,'head'=8] {'seq'}, dimensions={0}, use_global_device_ids=true | all-gather | bytes 532480 | tf_op jit(solution)/shard_map/all_gather | solution.py:226
  503.3 7.5 %while.32 = (s32[]{:T(128)}, f32[1,4,32]{2,1,0:T(4,128)S(1)}, f32[1,4,32]{2,1,0:T(4,128)S(1)}, f32[1,4,32,128]{3,2,1,0:T(8,128)S(1)}, s32[2]{0:T(128)S(1)}, /*in...) while((s32[]{:T(128)}, f32[1,4,32]{2,1,0:T(4,128)S(1)}, ...), condition=%wide.region_12.13_spmd.clone, body=%wide.region_7.12_spmd.clone.sunk | while | flops 68728680 | bytes 2437107 | solution.py:255
  504.7 1.3 compare_select_fusion.2
  508.4 1.3 compare_select_fusion.2
  512.1 58.5 %reduce-scatter.4.cloned.1.call-done = bf16[128,32]{1,0:T(8,128)(2,1)} async-done(((bf16[1024,32]{1,0:T(8,128)(2,1)}), bf16[128,32]{1,0:T(8,128)(2,1)}) %reduce-scatter.4.cloned.1.call-update) | async-done | bytes 8208
  (235 shorter events, 77.2 us)
Async XLA Ops:
  6.5 504.4 %copy-start = (bf16[512,1024]{1,0:T(8,128)(2,1)S(1)}, bf16[512,1024]{1,0:T(8,128)(2,1)}, u32[]{:S(2)}) copy-start(bf16[512,1024]{1,0:T(8,128)(2,1)} %param.41) | copy-start | bytes 3145732
  6.5 180.5 %copy-start.1 = (bf16[128,128]{1,0:T(8,128)(2,1)S(1)}, bf16[128,128]{1,0:T(8,128)(2,1)}, u32[]{:S(2)}) copy-start(bf16[128,128]{1,0:T(8,128)(2,1)} %param.27) | copy-start | bytes 98308
  6.5 180.8 %copy-start.8 = (f32[4]{0:T(128)S(1)}, f32[4]{0:T(128)}, u32[]{:S(2)}) copy-start(f32[4]{0:T(128)} %param.30) | copy-start | bytes 52
  6.5 181.2 %copy-start.4 = (bf16[128,256]{1,0:T(8,128)(2,1)S(1)}, bf16[128,256]{1,0:T(8,128)(2,1)}, u32[]{:S(2)}) copy-start(bf16[128,256]{1,0:T(8,128)(2,1)} %param.24) | copy-start | bytes 196612
  6.5 181.3 %copy-start.7 = (f32[256]{0:T(256)S(1)}, f32[256]{0:T(256)}, u32[]{:S(2)}) copy-start(f32[256]{0:T(256)} %param.31) | copy-start | bytes 3076
  6.5 181.3 %copy-start.6 = (bf16[256,1024]{1,0:T(8,128)(2,1)S(1)}, bf16[256,1024]{1,0:T(8,128)(2,1)}, u32[]{:S(2)}) copy-start(bf16[256,1024]{1,0:T(8,128)(2,1)} %param.32) | copy-start | bytes 1572868
  6.6 185.1 %copy-start.5 = (bf16[3072]{0:T(1024)(128)(2,1)S(1)}, bf16[3072]{0:T(1024)(128)(2,1)}, u32[]{:S(2)}) copy-start(bf16[3072]{0:T(1024)(128)(2,1)} %param.37) | copy-start | bytes 18436
  6.6 206.2 %copy-start.9 = (s32[1,32]{1,0:T(1,128)S(1)}, s32[1,32]{1,0:T(1,128)}, u32[]{:S(2)}) copy-start(s32[1,32]{1,0:T(1,128)} %param.34) | copy-start | bytes 388
  6.6 249.8 %copy-start.2 = (bf16[128,1024]{1,0:T(8,128)(2,1)S(1)}, bf16[128,1024]{1,0:T(8,128)(2,1)}, u32[]{:S(2)}) copy-start(bf16[128,1024]{1,0:T(8,128)(2,1)} %param.33) | copy-start | bytes 786436
  6.6 115.3 %all-gather.11.cloned.1.call-start = ((), (), s32[]{:S(2)}) async-start(), calls=%async_computation.4 | async-start | bytes 8519680 | tf_op jit(solution)/shard_map/all_gather | solution.py:28
  7.5 7.5 %collective-permute-start = (bf16[3,256]{1,0:T(4,128)(2,1)S(1)}, bf16[3,256]{1,0:T(4,128)(2,1)S(1)}, u32[]{:S(2)}, u32[]{:S(2)}) collective-permute-start(bf16[3,256]{1,0:T(4,128)(2,1)S(1)} %slice.52), channel_id=1, source_target_pairs={{0,8},{8,16},{16,24},{24,32},{32,40},{40,48},{48,56},{56,64},{64,7... | collective-permute-start | bytes 4616 | tf_op jit(solution)/shard_map/ppermute | solution.py:23
  15.8 324.5 %copy-start.3 = (f32[4096]{0:T(1024)S(1)}, f32[4096]{0:T(1024)}, u32[]{:S(2)}) copy-start(f32[4096]{0:T(1024)} %param.38) | copy-start | bytes 49156
  17.7 238.7 %all-reduce.5.cloned.1.call-start = ((), (), s32[]{:S(2)}) async-start(), calls=%async_computation.1 | async-start | bytes 524288 | tf_op jit(solution)/shard_map/psum | solution.py:163
  188.9 151.4 %all-gather.7.cloned.1.call-start = ((), (), s32[]{:S(2)}) async-start(), calls=%async_computation.2 | async-start | bytes 2129920 | tf_op jit(solution)/shard_map/all_gather | solution.py:204
  189.7 237.9 %all-gather.9.cloned.1.call-start = ((), (), s32[]{:S(2)}) async-start(), calls=%async_computation.3 | async-start | bytes 4259840 | tf_op jit(solution)/shard_map/all_gather | solution.py:199
  190.2 380.4 %reduce-scatter.4.cloned.1.call-start = ((), (), s32[]{:S(2)}) async-start(), calls=%async_computation.5 | async-start | bytes 294912
Sparse Core Ops, SparseCore 0:
  17.8 103.9 all-gather.10
  189.0 67.3 all-reduce.4
  259.9 80.3 all-gather.6
  343.6 83.9 all-gather.8
  512.2 58.3 reduce-scatter.3
where the time goes:
time: 581 us; the launch traced here: 579 us
  waiting for transfers between devices  334 us (57%)
  blocking collectives  129 us (22%)
  other arithmetic  70.1 us (12%)
  between operations  14.8 us (3%)
  matrix products  12.8 us (2%)
  local copies, waits for them, and re-layouts  9.55 us (2%)
    all_gather x1, waiting for transfers between devices, shards(): lax.all_gather(query_weight, 'seq', axis=0, tiled=True)  85.1 us
    all_gather x1, waiting for transfers between devices, shards(): lax.all_gather(key_value_weight, 'seq', axis=0, tiled=True)  82.5 us
    all_gather x1, waiting for transfers between devices, carried_in(): pieces = jax.tree.map(lambda part: lax.all_gather(part, axis), value)  62.9 us
    select_n x63, other arithmetic, step(): jnp.where(position < mine, new, old)  62.6 us
    unnamed x6, waiting for transfers between devices  59.8 us
    psum x1, waiting for transfers between devices, shards(): lax.psum(partial_enc.astype(jnp.bfloat16), 'head').astype(jnp.float32)  43.3 us
    all_gather x1, blocking collectives, carried_in(): pieces = jax.tree.map(lambda part: lax.all_gather(part, axis), value)  39 us
    all_gather x1, blocking collectives, shards(): value_rows = lax.all_gather(values, 'seq', axis=0, tiled=True)  36.1 us
  transfers between devices with their start and end apart: 6, of which 5 were waited for; matrix products, arithmetic and copies ran while one was open for 2% of the time, Pallas kernels for 0%

commit v1 on v0

v1 whole, which is shorter than its diff:
```python
import functools
import math

import jax
import jax.numpy as jnp
from jax import lax
from jax.experimental import pallas as pl
from jax.experimental.pallas import tpu as pltpu
from jax.sharding import PartitionSpec as P

F32 = jnp.float32
BF16 = jnp.bfloat16
MESH = pl.DeviceIdType.MESH
EXACT = lax.Precision.HIGHEST

NY = 8
NZ = 8
NHD = 8
L = 128
HEADS = 4
HP = 64
CAP = 32
HD = 128
D_MAIN = 4096
THETA = 500000.0
EPSILON = 1e-05

(
    STATS_Z,
    STATS_Y,
    W_AZ,
    W_BY,
    W_AY,
    W_BZ,
    SCAN1,
    SCAN2,
    SCAN3,
    SPAN_RS,
    SPAN_AG,
    ENC_RS,
    K_Z,
    V_Y,
    K_Y,
    V_Z,
    MAIN_RS,
    N_EX,
) = range(18)


def nn(a, b, precision=None):
    return lax.dot_general(
        a, b, (((1,), (0,)), ((), ())), precision=precision, preferred_element_type=F32
    )


def nt(a, b, precision=None):
    return lax.dot_general(
        a, b, (((1,), (1,)), ((), ())), precision=precision, preferred_element_type=F32
    )


def tn(a, b, precision=None):
    return lax.dot_general(
        a, b, (((0,), (0,)), ((), ())), precision=precision, preferred_element_type=F32
    )


def iota(shape, dim):
    return lax.broadcasted_iota(jnp.int32, shape, dim)


def silu(v):
    return v / (1.0 + jnp.exp(-v))


def one_minus_exp(u):
    series = u * (
        1.0
        - u
        * (
            1.0 / 2
            - u * (1.0 / 6 - u * (1.0 / 24 - u * (1.0 / 120 - u * (1.0 / 720 - u / 5040))))
        )
    )
    return jnp.where(u < 0.3, series, 1.0 - jnp.exp(-u))


def kernel(
    x_hbm,
    gate_hbm,
    convw_ref,
    b_hbm,
    c_hbm,
    step_ref,
    decay_ref,
    skip_ref,
    ngain_ref,
    mo_hbm,
    res_hbm,
    bnd_ref,
    cnt_ref,
    off_ref,
    pad_ref,
    mgain_ref,
    wq_hbm,
    wkv_hbm,
    mw_hbm,
    out_ref,
    x_ref,
    gate_ref,
    b_ref,
    c_ref,
    mo_ref,
    res_ref,
    wq_ref,
    wkv_ref,
    mw_ref,
    halo,
    ext,
    stats_z,
    stats_y,
    wbuf,
    s1_send,
    s1,
    s2,
    s3_send,
    s3,
    sp_send,
    sp_recv,
    ag,
    en_send,
    en_recv,
    kbuf,
    vbuf,
    mn_send,
    mn_recv,
    local_sem,
    halo_sem,
    w0_send,
    w0_recv,
    send_sem,
    recv_sem,
):
    s = lax.axis_index("seq")
    hd = lax.axis_index("head")
    y = s // NZ
    z = s % NZ

    def at_z(p):
        return (y * NZ + p, hd)

    def at_y(p):
        return (p * NZ + z, hd)

    def at_h(p):
        return (s, p)

    nxt = (lax.rem(s + 1, NY * NZ), hd)
    prv = (lax.rem(s + NY * NZ - 1, NY * NZ), hd)

    barrier = pltpu.get_barrier_semaphore()
    for d in range(1, 8):
        for to in (at_z(lax.rem(z + d, NZ)), at_y(lax.rem(y + d, NY)), at_h(lax.rem(hd + d, NHD))):
            pl.semaphore_signal(barrier, inc=1, device_id=to, device_id_type=MESH)
    pl.semaphore_signal(barrier, inc=1, device_id=prv, device_id_type=MESH)

    loads = [
        (b_hbm, b_ref),
        (c_hbm, c_ref),
        (wq_hbm, wq_ref),
        (wkv_hbm, wkv_ref),
        (x_hbm, x_ref),
        (gate_hbm, gate_ref),
        (mo_hbm, mo_ref),
        (res_hbm.at[:, pl.ds(pl.multiple_of(hd * 128, 128), 128)], res_ref),
        (mw_hbm, mw_ref),
    ]
    load = [pltpu.make_async_copy(a, b, local_sem.at[i]) for i, (a, b) in enumerate(loads)]
    for copy in load:
        copy.start()
    l_b, l_c, l_wq, l_wkv, l_x, l_gate, l_mo, l_res, l_mw = load

    pending = []

    def send_all(ex, me, where, src, dst):
        for d in range(1, 8):
            p = lax.rem(me + d, 8)
            copy = pltpu.make_async_remote_copy(
                src_ref=src(p),
                dst_ref=dst,
                send_sem=send_sem.at[ex, d],
                recv_sem=recv_sem.at[ex, me],
                device_id=where(p),
                device_id_type=MESH,
            )
            copy.start()
            pending.append(copy)

    def recv_all(ex, me, where, slot):
        for d in range(1, 8):
            p = lax.rem(me + 8 - d, 8)
            pltpu.make_async_remote_copy(
                src_ref=slot(p),
                dst_ref=slot(p),
                send_sem=send_sem.at[ex, d],
                recv_sem=recv_sem.at[ex, p],
                device_id=where(p),
                device_id_type=MESH,
            ).wait_recv()

    row4 = iota((HEADS, L), 0)
    coef = jnp.zeros((HEADS, L), F32)
    for h in range(HEADS):
        coef = jnp.where(row4 == h, decay_ref[h], coef)
    rate = step_ref[...] * coef
    log_decay = -rate
    gain_row = jnp.sqrt(one_minus_exp(2.0 * rate))
    ti = iota((L, L), 0)
    si = iota((L, L), 1)
    causal = ti >= si
    tri = jnp.where(causal, 1.0, 0.0).astype(F32)
    run_row = nt(log_decay, tri, EXACT)
    run_col = [
        nt(tri, jnp.broadcast_to(log_decay[h : h + 1, :], (L, L)), EXACT) for h in range(HEADS)
    ]
    rem_row = jnp.exp(run_row[:, L - 1 : L] - run_row) * gain_row
    first = si < HP
    eye = jnp.where(ti == si, 1.0, 0.0).astype(BF16)
    top = ti < HP
    rem_x = [
        nt(
            eye,
            jnp.where(
                top,
                jnp.broadcast_to(rem_row[2 * i : 2 * i + 1, :], (L, L)),
                jnp.broadcast_to(rem_row[2 * i + 1 : 2 * i + 2, :], (L, L)),
            ).astype(BF16),
        )
        for i in range(2)
    ]
    run_x = jnp.concatenate(
        [jnp.where(first, run_col[2 * i], run_col[2 * i + 1]) for i in range(2)], axis=1
    )

    l_wq.wait()
    l_wkv.wait()
    prow = s // 2 - 8
    padf = pad_ref[...].astype(F32)
    mg = mgain_ref[...]
    pad_one = jnp.sum(jnp.where(iota((24, 128), 0) == prow, padf, 0.0), axis=0, keepdims=True)
    gain_one = jnp.sum(jnp.where(iota((32, 128), 0) == s // 2, mg, 0.0), axis=0, keepdims=True)
    both = pad_one * gain_one
    half = jnp.where(s % 2 == 1, both[:, 64:], both[:, :64])
    half = jnp.broadcast_to(half, (16, 64)).astype(BF16)
    pq = nn(half, wq_ref[...])
    pkv = nn(half, wkv_ref[...])
    pad_sq = jnp.sum(jnp.sum(padf * padf, axis=1, keepdims=True), axis=0, keepdims=True)
    lane1 = iota((1, 128), 1)
    count = cnt_ref[0].astype(F32)
    last = jnp.zeros((1, 128), F32)
    for h in range(HEADS):
        last = jnp.where(lane1 == h, run_col[h][L - 1 : L, :], last)
    rows = [
        pq[0:1, 0:128],
        pq[0:1, 128:256],
        pkv[0:1, 0:128],
        pq[0:1, 256:384],
        pq[0:1, 384:512],
        pkv[0:1, 128:256],
        jnp.where(lane1 == z, count, 0.0),
        last,
    ]
    for i, row in enumerate(rows):
        stats_z[z, i : i + 1, :] = row

    pl.semaphore_wait(barrier, 22)

    halo_copy = pltpu.make_async_remote_copy(
        src_ref=x_hbm.at[pl.ds(L - 16, 16), :],
        dst_ref=halo,
        send_sem=halo_sem.at[0],
        recv_sem=halo_sem.at[1],
        device_id=nxt,
        device_id_type=MESH,
    )
    halo_copy.start()
    send_all(STATS_Z, z, at_z, lambda p: stats_z.at[z], stats_z.at[z])

    def w0_parts(yp):
        rg = lax.rem(yp, 4)
        ch = yp // 4
        r = pl.ds(pl.multiple_of(16 * rg, 16), 16)
        return (
            (
                wq_hbm.at[r, pl.ds(pl.multiple_of(256 * ch, 256), 256)],
                wbuf.at[ch, y, z, rg, :, pl.ds(0, 256)],
            ),
            (
                wkv_hbm.at[r, pl.ds(pl.multiple_of(128 * ch, 128), 128)],
                wbuf.at[ch, y, z, rg, :, pl.ds(256, 128)],
            ),
        )

    def w0_copies():
        copies = []
        for d in range(1, 8):
            yp = lax.rem(y + d, NY)
            for i, (src, dst) in enumerate(w0_parts(yp)):
                copies.append(
                    pltpu.make_async_remote_copy(
                        src_ref=src,
                        dst_ref=dst,
                        send_sem=w0_send.at[i, d],
                        recv_sem=w0_recv.at[i, y],
                        device_id=at_y(yp),
                        device_id_type=MESH,
                    )
                )
        return copies

    @pl.when(y < 2)
    def _():
        for copy in w0_copies():
            copy.start()
        for i, (src, dst) in enumerate(w0_parts(y)):
            pltpu.make_async_copy(src, dst, w0_recv.at[i, y]).start()

    l_b.wait()
    l_c.wait()
    bm = b_ref[...]
    cm = c_ref[...]
    affinity = jnp.where(causal, nt(cm, bm), 0.0)
    mix = []
    for h in range(HEADS):
        spread = jnp.where(causal, run_col[h] - run_row[h : h + 1, :], 0.0)
        mix.append((jnp.exp(spread) * (affinity * gain_row[h : h + 1, :])).astype(BF16))

    l_x.wait()
    halo_copy.wait()
    ext[16:, :] = x_ref[...].astype(F32)
    ext[0:16, :] = jnp.where(s == 0, 0.0, halo[...].astype(F32))
    cw = convw_ref[...]
    summed = cw[0:1, :] * ext[13 : 13 + L, :]
    for k in range(1, 4):
        summed = summed + cw[k : k + 1, :] * ext[13 + k : 13 + k + L, :]
    conv = silu(summed).astype(BF16)
    conv_f = conv.astype(F32)

    weighted = (conv_f * jnp.concatenate(rem_x, axis=1)).astype(BF16)
    state = tn(bm, weighted).astype(BF16)
    s1_send[...] = state.reshape(8, 16, 256)
    send_all(SCAN1, z, at_z, lambda p: s1_send.at[p], s1.at[z])
    s1[z] = s1_send[z]

    recv_all(STATS_Z, z, at_z, lambda p: stats_z.at[p])
    tiles = stats_z[...]
    stats_y[y] = jnp.sum(tiles, axis=0)
    send_all(STATS_Y, y, at_y, lambda p: stats_y.at[y], stats_y.at[y])

    for b in range(2):
        for i, (src, dst) in enumerate(w0_parts(y)):
            rg = lax.rem(y, 4)
            ch = y // 4
            cols = pl.ds(0, 256) if i == 0 else pl.ds(256, 128)
            slot = wbuf.at[ch, b, z, rg, :, cols]
            pltpu.make_async_copy(slot, slot, w0_recv.at[i, b]).wait()
    rg_me = lax.rem(y, 4)
    ch_me = y // 4
    send_all(
        W_AZ, z, at_z, lambda p: wbuf.at[ch_me, 0, z, rg_me], wbuf.at[ch_me, 0, z, rg_me]
    )
    send_all(
        W_BY, y, at_y, lambda p: wbuf.at[ch_me, 1, z, rg_me], wbuf.at[ch_me, 1, z, rg_me]
    )

    within = []
    zero = jnp.zeros((), BF16)
    for i in range(2):
        pair = conv[:, 128 * i : 128 * (i + 1)]
        stacked = jnp.concatenate(
            [jnp.where(first, pair, zero), jnp.where(first, zero, pair)], axis=0
        )
        within.append(nn(jnp.concatenate([mix[2 * i], mix[2 * i + 1]], axis=1), stacked))
    skip = jnp.zeros((1, 256), F32)
    head_of = iota((1, 256), 1) // HP
    for h in range(HEADS):
        skip = jnp.where(head_of == h, skip_ref[h], skip)
    mixed_near = jnp.concatenate(within, axis=1) + skip * conv_f
    exp_run = jnp.exp(run_x)
    l_gate.wait()
    gate = silu(gate_ref[...].astype(F32))

    spread_head = jnp.where(iota((128, 256), 0) == iota((128, 256), 1) // HP, 1.0, 0.0)
    spread_head = spread_head.astype(F32)
    lz = nn(tiles[:, 7, :], spread_head, EXACT)
    recv_all(SCAN1, z, at_z, lambda p: s1.at[p])
    acc = jnp.zeros((16, 256), F32)
    cum = jnp.zeros((1, 256), F32)
    before, cums = [], []
    for j in range(NZ):
        before.append(acc)
        cums.append(cum)
        acc = jnp.exp(lz[j : j + 1, :]) * acc + s1[j].astype(F32)
        cum = cum + lz[j : j + 1, :]
    s2[y] = acc.astype(BF16)
    send_all(SCAN2, y, at_y, lambda p: s2.at[y], s2.at[y])

    recv_all(STATS_Y, y, at_y, lambda p: stats_y.at[p])
    ytiles = stats_y[...]
    pad_total = jnp.sum(ytiles, axis=0)
    ly = nn(ytiles[:, 7, :], spread_head, EXACT)

    recv_all(W_AZ, z, at_z, lambda p: wbuf.at[ch_me, 0, p, rg_me])
    send_all(W_AY, y, at_y, lambda p: wbuf.at[ch_me, 0, :, rg_me], wbuf.at[ch_me, 0, :, rg_me])
    recv_all(W_BY, y, at_y, lambda p: wbuf.at[p // 4, 1, z, lax.rem(p, 4)])
    send_all(W_BZ, z, at_z, lambda p: wbuf.at[:, 1, z], wbuf.at[:, 1, z])

    recv_all(SCAN2, y, at_y, lambda p: s2.at[p])
    rows_before = jnp.zeros((16, 256), F32)
    for j in range(NY - 1):
        longer = jnp.exp(ly[j : j + 1, :]) * rows_before + s2[j].astype(F32)
        rows_before = jnp.where(j < y, longer, rows_before)
    for j in range(NZ):
        s3_send[j] = (before[j] + jnp.exp(cums[j]) * rows_before).astype(BF16)
    send_all(SCAN3, z, at_z, lambda p: s3_send.at[p], s3.at[z])
    s3[z] = s3_send[z]

    bnd = bnd_ref[...] - s * L
    byte_at = iota((L, CAP), 0)
    slot_at = iota((L, CAP), 1)
    usable = slot_at < cnt_ref[0]
    picker = jnp.where((byte_at == bnd) & usable, 1.0, 0.0).astype(BF16)
    upto = jnp.where((bnd <= byte_at) & usable, 1.0, 0.0)
    newest = jnp.sum(upto, axis=1, keepdims=True) - 1.0
    spreader = jnp.where(slot_at.astype(F32) == newest, 1.0, 0.0).astype(BF16)
    l_res.wait()
    res = res_ref[...]
    res_span = tn(picker, res)

    lane = iota((CAP, 128), 1)
    place = (iota((CAP, 128), 0) + off_ref[0]).astype(F32)
    freq = jnp.exp(
        lax.rem(lane, HD // 2).astype(F32) * (-2.0 * math.log(THETA) / HD)
    )
    angle = place * freq
    cosine = jnp.cos(angle)
    sine = jnp.where(lane < HD // 2, -jnp.sin(angle), jnp.sin(angle))

    recv_all(SCAN3, z, at_z, lambda p: s3.at[p])
    entering = nn(cm, s3[...].reshape(128, 256)) * exp_run
    gated = (mixed_near + entering) * gate
    mean_sq = jnp.sum(gated * gated, axis=1, keepdims=True) * (1.0 / 256)
    normed = (gated * lax.rsqrt(mean_sq + EPSILON) * ngain_ref[...]).astype(BF16)
    l_mo.wait()
    picked = tn(picker, normed).astype(BF16)
    span_part = nn(picked, mo_ref[...]).astype(BF16)
    for j in range(NHD):
        sp_send[j] = span_part[:, 128 * j : 128 * (j + 1)]
    send_all(SPAN_RS, hd, at_h, lambda p: sp_send.at[p], sp_recv.at[hd])
    sp_recv[hd] = sp_send[hd]
    enc_part = nn(normed, mo_ref[...]).astype(BF16)
    for j in range(NHD):
        en_send[j] = enc_part[:, 128 * j : 128 * (j + 1)]
    en_recv[hd] = en_send[hd]

    recv_all(SPAN_RS, hd, at_h, lambda p: sp_recv.at[p])
    span_share = (res_span + jnp.sum(sp_recv[...].astype(F32), axis=0)).astype(BF16)
    ag[hd] = span_share
    send_all(SPAN_AG, hd, at_h, lambda p: ag.at[hd], ag.at[hd])

    expand = jnp.where(
        iota((128, 2048), 0) == lax.rem(iota((128, 2048), 1) // CAP, NZ), 1.0, 0.0
    ).astype(BF16)
    per_row = nn(ytiles[:, 6, :].astype(BF16), expand)
    key_lane = iota((8, 2048), 1)
    counts = jnp.sum(
        jnp.where(key_lane // (CAP * NZ) == iota((8, 2048), 0), per_row, 0.0),
        axis=0,
        keepdims=True,
    )
    key1 = iota((1, 2048), 1)
    key_owner = key1 // CAP
    key_slot = key1 - key_owner * CAP
    known = key_slot.astype(F32) < counts
    limit = jnp.where(key_owner < s, -1, jnp.where(key_owner == s, key_slot, CAP))
    limit = jnp.where(known, limit, CAP)

    recv_all(SPAN_AG, hd, at_h, lambda p: ag.at[p])
    send_all(ENC_RS, hd, at_h, lambda p: en_send.at[p], en_recv.at[hd])
    sq = jnp.zeros((CAP, 1), F32)
    pieces = []
    for j in range(NHD):
        piece = ag[j].astype(F32)
        sq = sq + jnp.sum(piece * piece, axis=1, keepdims=True)
        pieces.append((piece * mg[j : j + 1, :]).astype(BF16))
    scale = lax.rsqrt((sq + pad_sq) * (1.0 / D_MAIN) + EPSILON)
    span_x = jnp.concatenate(pieces, axis=1)
    recv_all(W_AY, y, at_y, lambda p: wbuf.at[p // 4, 0, :, lax.rem(p, 4)])
    recv_all(W_BZ, z, at_z, lambda p: wbuf.at[:, 1, p])
    proj = [nn(span_x, wbuf[ch].reshape(1024, 384)) for ch in range(2)]

    def column(i):
        part = proj[i // 3][:, 128 * (i % 3) : 128 * (i % 3 + 1)]
        return (part + pad_total[i : i + 1, :]) * scale

    def rotate(v):
        return (v * cosine + pltpu.roll(v, HD // 2, 1) * sine).astype(BF16)

    kbuf[y, z] = rotate(column(2))
    vbuf[y, z] = column(5).astype(BF16)
    send_all(K_Z, z, at_z, lambda p: kbuf.at[y, z], kbuf.at[y, z])
    send_all(V_Y, y, at_y, lambda p: vbuf.at[y, z], vbuf.at[y, z])
    queries = jnp.concatenate([rotate(column(i)) for i in (0, 1, 3, 4)], axis=0)

    recv_all(K_Z, z, at_z, lambda p: kbuf.at[y, p])
    send_all(K_Y, y, at_y, lambda p: kbuf.at[y], kbuf.at[y])
    recv_all(V_Y, y, at_y, lambda p: vbuf.at[p, z])
    send_all(V_Z, z, at_z, lambda p: vbuf.at[:, z], vbuf.at[:, z])

    recv_all(ENC_RS, hd, at_h, lambda p: en_recv.at[p])
    encoded = (res.astype(F32) + jnp.sum(en_recv[...].astype(F32), axis=0)).astype(BF16)

    recv_all(K_Y, y, at_y, lambda p: kbuf.at[p])
    scores = nt(queries, kbuf[...].reshape(2048, HD)) * (1.0 / math.sqrt(HD))
    allowed = limit <= lax.rem(iota((128, 2048), 0), CAP)
    scores = jnp.where(allowed, scores, -1e30)
    highest = jnp.max(scores, axis=1, keepdims=True)
    weights = jnp.exp(scores - highest)
    total = jnp.sum(weights, axis=1, keepdims=True)
    recv_all(V_Z, z, at_z, lambda p: vbuf.at[:, p])
    attended = (nn(weights.astype(BF16), vbuf[...].reshape(2048, HD)) / total).astype(BF16)
    l_mw.wait()
    att = jnp.concatenate([attended[CAP * i : CAP * (i + 1), :] for i in range(4)], axis=1)
    main_part = nn(att, mw_ref[...]).astype(BF16)
    for j in range(NHD):
        mn_send[j] = main_part[:, 128 * j : 128 * (j + 1)]
    send_all(MAIN_RS, hd, at_h, lambda p: mn_send.at[p], mn_recv.at[hd])
    mn_recv[hd] = mn_send[hd]
    recv_all(MAIN_RS, hd, at_h, lambda p: mn_recv.at[p])
    main_rows = (span_share.astype(F32) + jnp.sum(mn_recv[...].astype(F32), axis=0)).astype(BF16)
    out_ref[...] = (encoded.astype(F32) + nn(spreader, main_rows)).astype(BF16)

    for copy in pending:
        copy.wait_send()

    @pl.when(y < 2)
    def _():
        for copy in w0_copies():
            copy.wait_send()


def shards(
    byte_stream,
    gate_stream,
    conv_weight,
    state_write,
    state_read,
    step_size,
    decay_coef,
    skip_gain,
    norm_gain,
    mixer_out,
    residual,
    boundaries,
    span_counts,
    span_offsets,
    pad_vector,
    main_gain,
    query_weight,
    key_value_weight,
    main_out_weight,
):
    far = pl.BlockSpec(memory_space=pl.ANY)
    near = pl.BlockSpec(memory_space=pltpu.VMEM)
    scalar = pl.BlockSpec(memory_space=pltpu.SMEM)
    vm = pltpu.VMEM
    dma = pltpu.SemaphoreType.DMA
    return pl.pallas_call(
        kernel,
        out_shape=jax.ShapeDtypeStruct((L, 128), BF16),
        in_specs=[
            far,
            far,
            near,
            far,
            far,
            near,
            scalar,
            scalar,
            near,
            far,
            far,
            near,
            scalar,
            scalar,
            near,
            near,
            far,
            far,
            far,
        ],
        out_specs=near,
        scratch_shapes=[
            vm((L, 256), BF16),
            vm((L, 256), BF16),
            vm((L, 128), BF16),
            vm((L, 128), BF16),
            vm((256, 1024), BF16),
            vm((L, 128), BF16),
            vm((64, 512), BF16),
            vm((64, 256), BF16),
            vm((512, 1024), BF16),
            vm((16, 256), BF16),
            vm((L + 16, 256), F32),
            vm((8, 8, 128), F32),
            vm((8, 8, 128), F32),
            vm((2, 2, 8, 4, 16, 384), BF16),
            vm((8, 16, 256), BF16),
            vm((8, 16, 256), BF16),
            vm((8, 16, 256), BF16),
            vm((8, 16, 256), BF16),
            vm((8, 16, 256), BF16),
            vm((8, CAP, 128), BF16),
            vm((8, CAP, 128), BF16),
            vm((8, CAP, 128), BF16),
            vm((8, L, 128), BF16),
            vm((8, L, 128), BF16),
            vm((8, 8, CAP, 128), BF16),
            vm((8, 8, CAP, 128), BF16),
            vm((8, CAP, 128), BF16),
            vm((8, CAP, 128), BF16),
            dma((9,)),
            dma((2,)),
            dma((2, 8)),
            dma((2, 2)),
            dma((N_EX, 8)),
            dma((N_EX, 8)),
        ],
        compiler_params=pltpu.CompilerParams(
            collective_id=0, has_side_effects=True, vmem_limit_bytes=40 * 1024 * 1024
        ),
        cost_estimate=pl.CostEstimate(flops=10**9, bytes_accessed=4 * 10**6, transcendentals=10**6),
    )(
        byte_stream,
        gate_stream,
        conv_weight,
        state_write,
        state_read,
        step_size.T,
        decay_coef,
        skip_gain,
        norm_gain.reshape(1, 256),
        mixer_out,
        residual,
        boundaries,
        span_counts,
        span_offsets,
        pad_vector.reshape(24, 128),
        main_gain.reshape(32, 128),
        query_weight,
        key_value_weight,
        main_out_weight,
    )


def solution(mesh):
    in_specs = (
        P("seq", "head"),
        P("seq", "head"),
        P(None, "head"),
        P("seq", None),
        P("seq", None),
        P("seq", "head"),
        P("head"),
        P("head"),
        P("head"),
        P("head", None),
        P("seq", None),
        P("seq", None),
        P("seq"),
        P("seq"),
        P(),
        P(),
        P("seq", "head"),
        P("seq", "head"),
        P("head", None),
    )
    out_specs = P("seq", "head")
    return jax.shard_map(shards, mesh=mesh, in_specs=in_specs, out_specs=out_specs, check_vma=False)
```

time: 581 us -> 96.6 us (0.17)
  waiting for transfers between devices: 334 us -> 0 us
  blocking collectives: 129 us -> 0 us
  Pallas kernels: 0 us -> 81.9 us
  other arithmetic: 70.1 us -> 0 us
  between operations: 14.8 us -> 1.36 us
  matrix products: 12.8 us -> 0 us
    all_gather x3 -> x0, waiting for transfers between devices: 231 us -> none  [the longest x1 85.1 us: shards(): lax.all_gather(query_weight, 'seq', axis=0, tiled=True)]
    all_gather x3 -> x0, blocking collectives: 111 us -> none  [the longest x1 39 us: carried_in(): pieces = jax.tree.map(lambda part: lax.all_gather(part, axis), value)]
    pallas_call x0 -> x1, Pallas kernels: none -> 81.9 us  [shards(): pl.pallas_call(kernel, out_shape=jax.ShapeDtypeStruct((L, 128), BF16), in...]
    select_n x69 -> x0, other arithmetic: 65.2 us -> none  [the longest x63 62.6 us: step(): jnp.where(position < mine, new, old)]
    unnamed x6 -> x0, waiting for transfers between devices: 59.8 us -> none
    psum x1 -> x0, waiting for transfers between devices: 43.3 us -> none  [shards(): lax.psum(partial_enc.astype(jnp.bfloat16), 'head').astype(jnp.float32)]
    unnamed x1 -> x0, blocking collectives: 18.3 us -> none
    dot_general x15 -> x0, matrix products: 12.8 us -> none  [the longest x1 3.05 us: shards(): jnp.dot(main_normed, lax.all_gather(query_weight, 'seq', axis=0, tiled=Tr...]
  transfers between devices with their start and end apart: 6 -> 0, of which waited for: 5 -> 0; matrix products, arithmetic and copies ran while one was open for 2% -> 0% of each run, Pallas kernels for 0% -> 0%
where the time goes in v1:
time: 96.6 us; the launch traced here: 95.9 us
  Pallas kernels  81.9 us (85%)
  local copies, waits for them, and re-layouts  12.7 us (13%)
  between operations  1.36 us (1%)
    pallas_call x1, Pallas kernels, shards(): pl.pallas_call(kernel, out_shape=jax.ShapeDtypeStruct((L, 128), BF16), in...  81.9 us
    unnamed x35, local copies, waits for them, and re-layouts  12.7 us

profile of v1, /device:TPU:1, one launch (start us, length us, event | category | flops | bytes accessed | tf_op | source)
XLA Modules:
  0.0 95.9 jit_solution(445423583199353723)
XLA Ops:
  0.0 0.0 copy-start.10
  1.3 0.0 copy-start.11
  1.3 0.0 copy-start.13
  1.3 0.0 copy-done.10
  1.3 0.7 copy-done.11
  2.0 0.0 copy-done.13
  2.0 1.2 %copy-done = bf16[512,1024]{1,0:T(8,128)(2,1)S(1)} copy-done((bf16[512,1024]{1,0:T(8,128)(2,1)S(1)}, bf16[512,1024]{1,0:T(8,128)(2,1)}, u32[]{:S(2)}) %copy-start) | copy-done | bytes 1048600
  3.2 0.0 copy-start.1
  3.2 1.0 %copy-done.1 = bf16[256,1024]{1,0:T(8,128)(2,1)S(1)} copy-done((bf16[256,1024]{1,0:T(8,128)(2,1)S(1)}, bf16[256,1024]{1,0:T(8,128)(2,1)}, u32[]{:S(2)}) %copy-start.1) | copy-done | bytes 524312
  4.3 0.0 copy-start.2
  4.3 0.9 copy-done.2
  5.2 0.8 copy-done.3
  6.1 0.8 copy-done.4
  6.9 0.8 copy-done.5
  7.7 0.8 copy-done.6
  8.5 0.8 copy-done.7
  9.3 0.8 copy-done.8
  10.0 0.7 copy-done.9
  10.7 0.7 copy-done.12
  11.4 0.7 copy-done.14
  12.1 0.7 copy-done.15
  12.7 0.7 copy-done.16
  13.4 81.9 %shard_map.181 = bf16[128,128]{1,0:T(8,128)(2,1)S(1)} custom-call(bf16[128,256]{1,0:T(8,128)(2,1)S(1)} %copy-done.3, bf16[128,256]{1,0:T(8,128)(2,1)S(1)} %copy-done.4, f32[4,256]{1,0:T(4,128)S(1)} %copy-done.11, bf16[128,128]{1,0:T(8,128)(2,1)S(1)} %copy-done.6, bf16[128,128]{1,0:T(8,128)(2,1)S(1)} %copy-done.7, f32[4,128]{1,0:T(4,128)S(1)} %bitcast.6, ...), custom_call_target="tpu_custom_call" | custom-call | flops 1000000000 | bytes 4000000 | tf_op jit(solution)/shard_map/pallas_call | solution.py:578
  95.3 0.6 copy.23
  (12 shorter events, 0.0 us)
Async XLA Ops:
  0.0 1.3 %copy-start.10 = (bf16[3072]{0:T(1024)(128)(2,1)S(1)}, bf16[3072]{0:T(1024)(128)(2,1)}, u32[]{:S(2)}) copy-start(bf16[3072]{0:T(1024)(128)(2,1)} %param.33) | copy-start | bytes 18436
  1.3 0.7 copy-start.11
  1.3 0.7 copy-start.13
  2.0 1.2 %copy-start = (bf16[512,1024]{1,0:T(8,128)(2,1)S(1)}, bf16[512,1024]{1,0:T(8,128)(2,1)}, u32[]{:S(2)}) copy-start(bf16[512,1024]{1,0:T(8,128)(2,1)} %mw_hbm.1) | copy-start | bytes 3145732
  3.2 1.0 %copy-start.1 = (bf16[256,1024]{1,0:T(8,128)(2,1)S(1)}, bf16[256,1024]{1,0:T(8,128)(2,1)}, u32[]{:S(2)}) copy-start(bf16[256,1024]{1,0:T(8,128)(2,1)} %mo_hbm.1) | copy-start | bytes 1572868
  4.3 0.9 copy-start.2
  5.2 0.8 copy-start.3
  6.1 0.8 copy-start.4
  6.9 0.8 copy-start.5
  7.7 0.8 copy-start.6
  8.5 0.8 copy-start.7
  9.3 0.8 copy-start.8
  10.0 0.7 copy-start.9
  10.7 0.7 copy-start.12
  11.4 0.7 copy-start.14
  12.1 0.7 copy-start.15
  12.7 0.7 copy-start.16

commit v2 on v1

--- a/solution.py
+++ b/solution.py
@@ -637,7 +637,7 @@
             dma((N_EX, 8)),
         ],
         compiler_params=pltpu.CompilerParams(
-            collective_id=0, has_side_effects=True, vmem_limit_bytes=40 * 1024 * 1024
+            collective_id=0, has_side_effects=True, vmem_limit_bytes=56 * 1024 * 1024
         ),
         cost_estimate=pl.CostEstimate(flops=10**9, bytes_accessed=4 * 10**6, transcendentals=10**6),
     )(

time: 96.6 us -> 85.3 us (0.88)
  local copies, waits for them, and re-layouts: 12.7 us -> 1.38 us
    unnamed x35 -> x1, local copies, waits for them, and re-layouts: 12.7 us -> 1.38 us
where the time goes in v2:
time: 85.3 us; the launch traced here: 85 us
  Pallas kernels  82.3 us (96%)
  local copies, waits for them, and re-layouts  1.38 us (2%)
  between operations  1.3 us (2%)
    pallas_call x1, Pallas kernels, shards(): pl.pallas_call(kernel, out_shape=jax.ShapeDtypeStruct((L, 128), BF16), in...  82.3 us

profile of v2, /device:TPU:1, one launch (start us, length us, event | category | flops | bytes accessed | tf_op | source)
XLA Modules:
  0.0 85.0 jit_solution(17049138333814083468)
XLA Ops:
  1.3 82.3 %shard_map.181 = bf16[128,128]{1,0:T(8,128)(2,1)} custom-call(bf16[128,256]{1,0:T(8,128)(2,1)} %x_hbm.1, bf16[128,256]{1,0:T(8,128)(2,1)} %gate_hbm.1, f32[4,256]{1,0:T(4,128)} %convw_ref.1, bf16[128,128]{1,0:T(8,128)(2,1)} %b_hbm.1, bf16[128,128]{1,0:T(8,128)(2,1)} %c_hbm.1, f32[4,128]{1,0:T(4,128)} %bitcast.6, f32[4]{0:T(128)} %decay_ref.1, f32[4]{0:T(128)} %skip_ref.1, ...), custom_call_target="tpu_custom_call" | custom-call | flops 1000000000 | bytes 4000000 | tf_op jit(solution)/shard_map/pallas_call | solution.py:578
  83.6 1.4 %copy.23 = bf16[128,128]{1,0:T(8,128)(2,1)} copy(bf16[128,128]{1,0:T(8,128)(2,1)} %shard_map.181) | data formatting | bytes 65536

commit v3 on v2

--- a/solution.py
+++ b/solution.py
@@ -30,21 +30,17 @@
     STATS_Y,
     W_AZ,
     W_BY,
-    W_AY,
-    W_BZ,
+    RING_A,
+    RING_B,
     SCAN1,
     SCAN2,
     SCAN3,
     SPAN_RS,
     SPAN_AG,
     ENC_RS,
-    K_Z,
-    V_Y,
-    K_Y,
-    V_Z,
     MAIN_RS,
     N_EX,
-) = range(18)
+) = range(14)
 
 
 def nn(a, b, precision=None):
@@ -130,14 +126,21 @@
     ag,
     en_send,
     en_recv,
-    kbuf,
-    vbuf,
+    kvbuf,
+    qbuf,
+    key_ranks,
+    o_send,
+    m_send,
+    o_recv,
+    m_recv,
     mn_send,
     mn_recv,
     local_sem,
     halo_sem,
     w0_send,
     w0_recv,
+    kv_sem,
+    group_sem,
     send_sem,
     recv_sem,
 ):
@@ -158,18 +161,34 @@
     nxt = (lax.rem(s + 1, NY * NZ), hd)
     prv = (lax.rem(s + NY * NZ - 1, NY * NZ), hd)
 
+    py, pz = lax.rem(y, 2), lax.rem(z, 2)
+    yi, zi = y // 2, z // 2
+
+    def at_class(dy, dz):
+        yc, zc = 2 * lax.rem(yi + dy, 4) + py, 2 * lax.rem(zi + dz, 4) + pz
+        return (yc * NZ + zc, hd)
+
+    def member(e):
+        yc = y + 1 - 2 * py if e // 2 else y
+        zc = z + 1 - 2 * pz if e % 2 else z
+        return (yc * NZ + zc, hd), 2 * lax.rem(yc, 2) + lax.rem(zc, 2)
+
     barrier = pltpu.get_barrier_semaphore()
+    greet = [prv, member(3)[0]]
     for d in range(1, 8):
-        for to in (at_z(lax.rem(z + d, NZ)), at_y(lax.rem(y + d, NY)), at_h(lax.rem(hd + d, NHD))):
-            pl.semaphore_signal(barrier, inc=1, device_id=to, device_id_type=MESH)
-    pl.semaphore_signal(barrier, inc=1, device_id=prv, device_id_type=MESH)
+        greet += [at_z(lax.rem(z + d, NZ)), at_y(lax.rem(y + d, NY)), at_h(lax.rem(hd + d, NHD))]
+    for dy in range(1, 4):
+        for dz in range(1, 4):
+            greet.append(at_class(dy, dz))
+    for to in greet:
+        pl.semaphore_signal(barrier, inc=1, device_id=to, device_id_type=MESH)
 
     loads = [
         (b_hbm, b_ref),
         (c_hbm, c_ref),
+        (x_hbm, x_ref),
         (wq_hbm, wq_ref),
         (wkv_hbm, wkv_ref),
-        (x_hbm, x_ref),
         (gate_hbm, gate_ref),
         (mo_hbm, mo_ref),
         (res_hbm.at[:, pl.ds(pl.multiple_of(hd * 128, 128), 128)], res_ref),
@@ -178,7 +197,7 @@
     load = [pltpu.make_async_copy(a, b, local_sem.at[i]) for i, (a, b) in enumerate(loads)]
     for copy in load:
         copy.start()
-    l_b, l_c, l_wq, l_wkv, l_x, l_gate, l_mo, l_res, l_mw = load
+    l_b, l_c, l_x, l_wq, l_wkv, l_gate, l_mo, l_res, l_mw = load
 
     pending = []
 
@@ -242,6 +261,67 @@
         [jnp.where(first, run_col[2 * i], run_col[2 * i + 1]) for i in range(2)], axis=1
     )
 
+    pl.semaphore_wait(barrier, len(greet))
+
+    halo_copy = pltpu.make_async_remote_copy(
+        src_ref=x_hbm.at[pl.ds(L - 16, 16), :],
+        dst_ref=halo,
+        send_sem=halo_sem.at[0],
+        recv_sem=halo_sem.at[1],
+        device_id=nxt,
+        device_id_type=MESH,
+    )
+    halo_copy.start()
+
+    def w0_parts(yp):
+        rg = lax.rem(yp, 4)
+        ch = yp // 4
+        r = pl.ds(pl.multiple_of(16 * rg, 16), 16)
+        return (
+            (
+                wq_hbm.at[r, pl.ds(pl.multiple_of(256 * ch, 256), 256)],
+                wbuf.at[ch, y, z, rg, :, pl.ds(0, 256)],
+            ),
+            (
+                wkv_hbm.at[r, pl.ds(pl.multiple_of(128 * ch, 128), 128)],
+                wbuf.at[ch, y, z, rg, :, pl.ds(256, 128)],
+            ),
+        )
+
+    def w0_copies():
+        copies = []
+        for d in range(1, 8):
+            yp = lax.rem(y + d, NY)
+            for i, (src, dst) in enumerate(w0_parts(yp)):
+                copies.append(
+                    pltpu.make_async_remote_copy(
+                        src_ref=src,
+                        dst_ref=dst,
+                        send_sem=w0_send.at[i, d],
+                        recv_sem=w0_recv.at[i, y],
+                        device_id=at_y(yp),
+                        device_id_type=MESH,
+                    )
+                )
+        return copies
+
+    @pl.when(y < 2)
+    def _():
+        for copy in w0_copies():
+            copy.start()
+        for i, (src, dst) in enumerate(w0_parts(y)):
+            pltpu.make_async_copy(src, dst, w0_recv.at[i, y]).start()
+
+    l_b.wait()
+    l_c.wait()
+    bm = b_ref[...]
+    cm = c_ref[...]
+    affinity = jnp.where(causal, nt(cm, bm), 0.0)
+    mix = []
+    for h in range(HEADS):
+        spread = jnp.where(causal, run_col[h] - run_row[h : h + 1, :], 0.0)
+        mix.append((jnp.exp(spread) * (affinity * gain_row[h : h + 1, :])).astype(BF16))
+
     l_wq.wait()
     l_wkv.wait()
     prow = s // 2 - 8
@@ -272,68 +352,7 @@
     ]
     for i, row in enumerate(rows):
         stats_z[z, i : i + 1, :] = row
-
-    pl.semaphore_wait(barrier, 22)
-
-    halo_copy = pltpu.make_async_remote_copy(
-        src_ref=x_hbm.at[pl.ds(L - 16, 16), :],
-        dst_ref=halo,
-        send_sem=halo_sem.at[0],
-        recv_sem=halo_sem.at[1],
-        device_id=nxt,
-        device_id_type=MESH,
-    )
-    halo_copy.start()
     send_all(STATS_Z, z, at_z, lambda p: stats_z.at[z], stats_z.at[z])
-
-    def w0_parts(yp):
-        rg = lax.rem(yp, 4)
-        ch = yp // 4
-        r = pl.ds(pl.multiple_of(16 * rg, 16), 16)
-        return (
-            (
-                wq_hbm.at[r, pl.ds(pl.multiple_of(256 * ch, 256), 256)],
-                wbuf.at[ch, y, z, rg, :, pl.ds(0, 256)],
-            ),
-            (
-                wkv_hbm.at[r, pl.ds(pl.multiple_of(128 * ch, 128), 128)],
-                wbuf.at[ch, y, z, rg, :, pl.ds(256, 128)],
-            ),
-        )
-
-    def w0_copies():
-        copies = []
-        for d in range(1, 8):
-            yp = lax.rem(y + d, NY)
-            for i, (src, dst) in enumerate(w0_parts(yp)):
-                copies.append(
-                    pltpu.make_async_remote_copy(
-                        src_ref=src,
-                        dst_ref=dst,
-                        send_sem=w0_send.at[i, d],
-                        recv_sem=w0_recv.at[i, y],
-                        device_id=at_y(yp),
-                        device_id_type=MESH,
-                    )
-                )
-        return copies
-
-    @pl.when(y < 2)
-    def _():
-        for copy in w0_copies():
-            copy.start()
-        for i, (src, dst) in enumerate(w0_parts(y)):
-            pltpu.make_async_copy(src, dst, w0_recv.at[i, y]).start()
-
-    l_b.wait()
-    l_c.wait()
-    bm = b_ref[...]
-    cm = c_ref[...]
-    affinity = jnp.where(causal, nt(cm, bm), 0.0)
-    mix = []
-    for h in range(HEADS):
-        spread = jnp.where(causal, run_col[h] - run_row[h : h + 1, :], 0.0)
-        mix.append((jnp.exp(spread) * (affinity * gain_row[h : h + 1, :])).astype(BF16))
 
     l_x.wait()
     halo_copy.wait()
@@ -405,15 +424,47 @@
     s2[y] = acc.astype(BF16)
     send_all(SCAN2, y, at_y, lambda p: s2.at[y], s2.at[y])
 
+    def block_a(p, lo=0, n=8):
+        return wbuf.at[p // 4, 0, pl.ds(lo, n), lax.rem(p, 4)]
+
+    def block_b(p, lo=0, n=2):
+        return wbuf.at[pl.ds(lo, n), 1, p]
+
+    def rings(step, wait):
+        for ex, me, where, block, whole in (
+            (RING_A, y, at_y, block_a, 8),
+            (RING_B, z, at_z, block_b, 2),
+        ):
+            for way in range(2):
+                ahead = lax.rem(me + (1 if way == 0 else 7), 8)
+                moved = step + (1 if wait else 0)
+                of = lax.rem(me + (8 - moved if way == 0 else moved), 8)
+                if step == 3:
+                    part = block(of, way * whole // 2, whole // 2)
+                else:
+                    part = block(of)
+                copy = pltpu.make_async_remote_copy(
+                    src_ref=part,
+                    dst_ref=part,
+                    send_sem=send_sem.at[ex, 2 * step + way],
+                    recv_sem=recv_sem.at[ex, 2 * step + way],
+                    device_id=where(ahead),
+                    device_id_type=MESH,
+                )
+                if wait:
+                    copy.wait_recv()
+                else:
+                    copy.start()
+                    pending.append(copy)
+
+    recv_all(W_AZ, z, at_z, lambda p: wbuf.at[ch_me, 0, p, rg_me])
+    recv_all(W_BY, y, at_y, lambda p: wbuf.at[p // 4, 1, z, lax.rem(p, 4)])
+    rings(0, False)
+
     recv_all(STATS_Y, y, at_y, lambda p: stats_y.at[p])
     ytiles = stats_y[...]
     pad_total = jnp.sum(ytiles, axis=0)
     ly = nn(ytiles[:, 7, :], spread_head, EXACT)
-
-    recv_all(W_AZ, z, at_z, lambda p: wbuf.at[ch_me, 0, p, rg_me])
-    send_all(W_AY, y, at_y, lambda p: wbuf.at[ch_me, 0, :, rg_me], wbuf.at[ch_me, 0, :, rg_me])
-    recv_all(W_BY, y, at_y, lambda p: wbuf.at[p // 4, 1, z, lax.rem(p, 4)])
-    send_all(W_BZ, z, at_z, lambda p: wbuf.at[:, 1, z], wbuf.at[:, 1, z])
 
     recv_all(SCAN2, y, at_y, lambda p: s2.at[p])
     rows_before = jnp.zeros((16, 256), F32)
@@ -424,6 +475,9 @@
         s3_send[j] = (before[j] + jnp.exp(cums[j]) * rows_before).astype(BF16)
     send_all(SCAN3, z, at_z, lambda p: s3_send.at[p], s3.at[z])
     s3[z] = s3_send[z]
+
+    rings(0, True)
+    rings(1, False)
 
     bnd = bnd_ref[...] - s * L
     byte_at = iota((L, CAP), 0)
@@ -458,6 +512,10 @@
         sp_send[j] = span_part[:, 128 * j : 128 * (j + 1)]
     send_all(SPAN_RS, hd, at_h, lambda p: sp_send.at[p], sp_recv.at[hd])
     sp_recv[hd] = sp_send[hd]
+
+    rings(1, True)
+    rings(2, False)
+
     enc_part = nn(normed, mo_ref[...]).astype(BF16)
     for j in range(NHD):
         en_send[j] = enc_part[:, 128 * j : 128 * (j + 1)]
@@ -468,22 +526,28 @@
     ag[hd] = span_share
     send_all(SPAN_AG, hd, at_h, lambda p: ag.at[hd], ag.at[hd])
 
-    expand = jnp.where(
-        iota((128, 2048), 0) == lax.rem(iota((128, 2048), 1) // CAP, NZ), 1.0, 0.0
-    ).astype(BF16)
-    per_row = nn(ytiles[:, 6, :].astype(BF16), expand)
-    key_lane = iota((8, 2048), 1)
-    counts = jnp.sum(
-        jnp.where(key_lane // (CAP * NZ) == iota((8, 2048), 0), per_row, 0.0),
-        axis=0,
+    rings(2, True)
+    rings(3, False)
+
+    key = iota((512, 128), 0)
+    key_y, key_z = 2 * (key // 128) + py, 2 * lax.rem(key // CAP, 4) + pz
+    expand = jnp.where(iota((512, 128), 1) == key_z, 1.0, 0.0).astype(BF16)
+    per_row = nt(expand, jnp.concatenate([ytiles[:, 6, :], ytiles[:, 6, :]], axis=0).astype(BF16))
+    lane16 = iota((512, 16), 1)
+    key_count = jnp.sum(
+        jnp.where(lane16 == 2 * (iota((512, 16), 0) // 128) + py, per_row, 0.0),
+        axis=1,
         keepdims=True,
     )
-    key1 = iota((1, 2048), 1)
-    key_owner = key1 // CAP
-    key_slot = key1 - key_owner * CAP
-    known = key_slot.astype(F32) < counts
-    limit = jnp.where(key_owner < s, -1, jnp.where(key_owner == s, key_slot, CAP))
-    limit = jnp.where(known, limit, CAP)
+    key_slot = lax.rem(key, CAP)
+    key_rank = (key_y * NZ + key_z) * CAP + key_slot
+    key_rank = jnp.where(key_slot.astype(F32) < key_count, key_rank, NY * NZ * CAP)
+    key_ranks[...] = key_rank
+    query = iota((1, 512), 1)
+    query_rank = (
+        ((y - py + query // 256) * NZ + z - pz + lax.rem(query // 128, 2)) * CAP
+        + lax.rem(query, CAP)
+    )
 
     recv_all(SPAN_AG, hd, at_h, lambda p: ag.at[p])
     send_all(ENC_RS, hd, at_h, lambda p: en_send.at[p], en_recv.at[hd])
@@ -495,8 +559,7 @@
         pieces.append((piece * mg[j : j + 1, :]).astype(BF16))
     scale = lax.rsqrt((sq + pad_sq) * (1.0 / D_MAIN) + EPSILON)
     span_x = jnp.concatenate(pieces, axis=1)
-    recv_all(W_AY, y, at_y, lambda p: wbuf.at[p // 4, 0, :, lax.rem(p, 4)])
-    recv_all(W_BZ, z, at_z, lambda p: wbuf.at[:, 1, p])
+    rings(3, True)
     proj = [nn(span_x, wbuf[ch].reshape(1024, 384)) for ch in range(2)]
 
     def column(i):
@@ -506,29 +569,99 @@
     def rotate(v):
         return (v * cosine + pltpu.roll(v, HD // 2, 1) * sine).astype(BF16)
 
-    kbuf[y, z] = rotate(column(2))
-    vbuf[y, z] = column(5).astype(BF16)
-    send_all(K_Z, z, at_z, lambda p: kbuf.at[y, z], kbuf.at[y, z])
-    send_all(V_Y, y, at_y, lambda p: vbuf.at[y, z], vbuf.at[y, z])
-    queries = jnp.concatenate([rotate(column(i)) for i in (0, 1, 3, 4)], axis=0)
-
-    recv_all(K_Z, z, at_z, lambda p: kbuf.at[y, p])
-    send_all(K_Y, y, at_y, lambda p: kbuf.at[y], kbuf.at[y])
-    recv_all(V_Y, y, at_y, lambda p: vbuf.at[p, z])
-    send_all(V_Z, z, at_z, lambda p: vbuf.at[:, z], vbuf.at[:, z])
+    kvbuf[yi, zi, 0] = rotate(column(2))
+    kvbuf[yi, zi, 1] = column(5).astype(BF16)
+    kv_copies = []
+    for dy in range(4):
+        for dz in range(4):
+            if dy + dz > 0:
+                kv_copies.append(
+                    pltpu.make_async_remote_copy(
+                        src_ref=kvbuf.at[yi, zi],
+                        dst_ref=kvbuf.at[yi, zi],
+                        send_sem=kv_sem.at[0, 4 * dy + dz],
+                        recv_sem=kv_sem.at[1, 4 * dy + dz],
+                        device_id=at_class(dy, dz),
+                        device_id_type=MESH,
+                    )
+                )
+    for copy in kv_copies:
+        copy.start()
+        pending.append(copy)
+    mine = 2 * py + pz
+    qbuf[mine] = jnp.concatenate([rotate(column(i)) for i in (0, 1, 3, 4)], axis=0)
+
+    def group_copy(i, e, src, dst):
+        return pltpu.make_async_remote_copy(
+            src_ref=src,
+            dst_ref=dst,
+            send_sem=group_sem.at[0, i, e],
+            recv_sem=group_sem.at[1, i, e],
+            device_id=member(e)[0],
+            device_id_type=MESH,
+        )
+
+    for e in range(1, 4):
+        copy = group_copy(0, e, qbuf.at[mine], qbuf.at[mine])
+        copy.start()
+        pending.append(copy)
 
     recv_all(ENC_RS, hd, at_h, lambda p: en_recv.at[p])
     encoded = (res.astype(F32) + jnp.sum(en_recv[...].astype(F32), axis=0)).astype(BF16)
 
-    recv_all(K_Y, y, at_y, lambda p: kbuf.at[p])
-    scores = nt(queries, kbuf[...].reshape(2048, HD)) * (1.0 / math.sqrt(HD))
-    allowed = limit <= lax.rem(iota((128, 2048), 0), CAP)
-    scores = jnp.where(allowed, scores, -1e30)
-    highest = jnp.max(scores, axis=1, keepdims=True)
-    weights = jnp.exp(scores - highest)
-    total = jnp.sum(weights, axis=1, keepdims=True)
-    recv_all(V_Z, z, at_z, lambda p: vbuf.at[:, p])
-    attended = (nn(weights.astype(BF16), vbuf[...].reshape(2048, HD)) / total).astype(BF16)
+    for e in range(1, 4):
+        slot = qbuf.at[member(e)[1]]
+        group_copy(0, e, slot, slot).wait_recv()
+    for dy in range(4):
+        for dz in range(4):
+            if dy + dz > 0:
+                slot = kvbuf.at[lax.rem(yi + 4 - dy, 4), lax.rem(zi + 4 - dz, 4)]
+                pltpu.make_async_remote_copy(
+                    src_ref=slot,
+                    dst_ref=slot,
+                    send_sem=kv_sem.at[0, 4 * dy + dz],
+                    recv_sem=kv_sem.at[1, 4 * dy + dz],
+                    device_id=at_class(dy, dz),
+                    device_id_type=MESH,
+                ).wait_recv()
+
+    kv = kvbuf[...]
+    keys = kv[:, :, 0].reshape(512, HD)
+    values = kv[:, :, 1].reshape(512, HD)
+    ranks = key_ranks[...]
+    unit = 1.0 / math.sqrt(HD)
+    for m in range(4):
+        scores = nt(keys, qbuf[m])
+        allowed = ranks <= query_rank[:, 128 * m : 128 * (m + 1)]
+        scores = jnp.where(allowed, scores * unit, -1e30)
+        top = jnp.max(scores, axis=0, keepdims=True)
+        weights = jnp.exp(scores - top)
+        o_send[m] = tn(values, weights.astype(BF16)).astype(BF16)
+        m_send[m, 0:1, :] = top
+        m_send[m, 1:2, :] = jnp.sum(weights, axis=0, keepdims=True)
+
+    for e in range(1, 4):
+        place_e = member(e)[1]
+        for i, (src, dst) in enumerate(((o_send, o_recv), (m_send, m_recv))):
+            copy = group_copy(1 + i, e, src.at[place_e], dst.at[e])
+            copy.start()
+            pending.append(copy)
+    o_recv[0] = o_send[mine]
+    m_recv[0] = m_send[mine]
+
+    for e in range(1, 4):
+        group_copy(1, e, o_recv.at[e], o_recv.at[e]).wait_recv()
+        group_copy(2, e, m_recv.at[e], m_recv.at[e]).wait_recv()
+
+    tops = m_recv[:, 0, :]
+    highest = jnp.max(tops, axis=0, keepdims=True)
+    shrink = jnp.exp(tops - highest)
+    total = jnp.sum(shrink * m_recv[:, 1, :], axis=0, keepdims=True)
+    summed_o = jnp.zeros((HD, 128), F32)
+    for e in range(4):
+        summed_o = summed_o + shrink[e : e + 1, :] * o_recv[e].astype(F32)
+    attended = (summed_o / total).T.astype(BF16)
+
     l_mw.wait()
     att = jnp.concatenate([attended[CAP * i : CAP * (i + 1), :] for i in range(4)], axis=1)
     main_part = nn(att, mw_ref[...]).astype(BF16)
@@ -625,14 +758,21 @@
             vm((8, CAP, 128), BF16),
             vm((8, L, 128), BF16),
             vm((8, L, 128), BF16),
-            vm((8, 8, CAP, 128), BF16),
-            vm((8, 8, CAP, 128), BF16),
+            vm((4, 4, 2, CAP, 128), BF16),
+            vm((4, 128, 128), BF16),
+            vm((512, 128), jnp.int32),
+            vm((4, 128, 128), BF16),
+            vm((4, 8, 128), F32),
+            vm((4, 128, 128), BF16),
+            vm((4, 8, 128), F32),
             vm((8, CAP, 128), BF16),
             vm((8, CAP, 128), BF16),
             dma((9,)),
             dma((2,)),
             dma((2, 8)),
             dma((2, 2)),
+            dma((2, 16)),
+            dma((2, 3, 4)),
             dma((N_EX, 8)),
             dma((N_EX, 8)),
         ],

time: 85.3 us -> 74 us (0.87)
  Pallas kernels: 82.3 us -> 71.1 us
    pallas_call x1, Pallas kernels: 82.3 us -> 71.1 us  [shards(): pl.pallas_call(kernel, out_shape=jax.ShapeDtypeStruct((L, 128), BF16), in...]
where the time goes in v3:
time: 74 us; the launch traced here: 73.8 us
  Pallas kernels  71.1 us (96%)
  local copies, waits for them, and re-layouts  1.38 us (2%)
  between operations  1.3 us (2%)
    pallas_call x1, Pallas kernels, shards(): pl.pallas_call(kernel, out_shape=jax.ShapeDtypeStruct((L, 128), BF16), in...  71.1 us

profile of v3, /device:TPU:1, one launch (start us, length us, event | category | flops | bytes accessed | tf_op | source)
XLA Modules:
  0.0 73.8 jit_solution(7865599475144797225)
XLA Ops:
  1.3 71.1 %shard_map.181 = bf16[128,128]{1,0:T(8,128)(2,1)} custom-call(bf16[128,256]{1,0:T(8,128)(2,1)} %x_hbm.1, bf16[128,256]{1,0:T(8,128)(2,1)} %gate_hbm.1, f32[4,256]{1,0:T(4,128)} %convw_ref.1, bf16[128,128]{1,0:T(8,128)(2,1)} %b_hbm.1, bf16[128,128]{1,0:T(8,128)(2,1)} %c_hbm.1, f32[4,128]{1,0:T(4,128)} %bitcast.6, f32[4]{0:T(128)} %decay_ref.1, f32[4]{0:T(128)} %skip_ref.1, ...), custom_call_target="tpu_custom_call" | custom-call | flops 1000000000 | bytes 4000000 | tf_op jit(solution)/shard_map/pallas_call | solution.py:711
  72.4 1.4 %copy.23 = bf16[128,128]{1,0:T(8,128)(2,1)} copy(bf16[128,128]{1,0:T(8,128)(2,1)} %shard_map.181) | data formatting | bytes 65536

commit v4 on v3

--- a/solution.py
+++ b/solution.py
@@ -24,6 +24,8 @@
 D_MAIN = 4096
 THETA = 500000.0
 EPSILON = 1e-05
+FAR_FIRST = (4, 3, 5, 2, 6, 1, 7)
+SLOTS = sorted(((i, j) for i in range(4) for j in range(4) if i + j > 0), key=lambda t: -t[0] - t[1])
 
 (
     STATS_Z,
@@ -162,10 +164,11 @@
     prv = (lax.rem(s + NY * NZ - 1, NY * NZ), hd)
 
     py, pz = lax.rem(y, 2), lax.rem(z, 2)
-    yi, zi = y // 2, z // 2
-
-    def at_class(dy, dz):
-        yc, zc = 2 * lax.rem(yi + dy, 4) + py, 2 * lax.rem(zi + dz, 4) + pz
+    sy, sz = 1 - 2 * py, 1 - 2 * pz
+
+    def at_slot(i, j):
+        yc = lax.rem(y + 8 + (0, -1, 2, -3)[i] * sy, NY)
+        zc = lax.rem(z + 8 + (0, -1, 2, -3)[j] * sz, NZ)
         return (yc * NZ + zc, hd)
 
     def member(e):
@@ -174,12 +177,9 @@
         return (yc * NZ + zc, hd), 2 * lax.rem(yc, 2) + lax.rem(zc, 2)
 
     barrier = pltpu.get_barrier_semaphore()
-    greet = [prv, member(3)[0]]
+    greet = [prv]
     for d in range(1, 8):
         greet += [at_z(lax.rem(z + d, NZ)), at_y(lax.rem(y + d, NY)), at_h(lax.rem(hd + d, NHD))]
-    for dy in range(1, 4):
-        for dz in range(1, 4):
-            greet.append(at_class(dy, dz))
     for to in greet:
         pl.semaphore_signal(barrier, inc=1, device_id=to, device_id_type=MESH)
 
@@ -202,7 +202,7 @@
     pending = []
 
     def send_all(ex, me, where, src, dst):
-        for d in range(1, 8):
+        for d in FAR_FIRST:
             p = lax.rem(me + d, 8)
             copy = pltpu.make_async_remote_copy(
                 src_ref=src(p),
@@ -290,7 +290,7 @@
 
     def w0_copies():
         copies = []
-        for d in range(1, 8):
+        for d in FAR_FIRST:
             yp = lax.rem(y + d, NY)
             for i, (src, dst) in enumerate(w0_parts(yp)):
                 copies.append(
@@ -530,12 +530,13 @@
     rings(3, False)
 
     key = iota((512, 128), 0)
-    key_y, key_z = 2 * (key // 128) + py, 2 * lax.rem(key // CAP, 4) + pz
+    key_y = lax.rem(y + 16 - (key // 128) * sy, NY)
+    key_z = lax.rem(z + 16 - lax.rem(key // CAP, 4) * sz, NZ)
     expand = jnp.where(iota((512, 128), 1) == key_z, 1.0, 0.0).astype(BF16)
     per_row = nt(expand, jnp.concatenate([ytiles[:, 6, :], ytiles[:, 6, :]], axis=0).astype(BF16))
     lane16 = iota((512, 16), 1)
     key_count = jnp.sum(
-        jnp.where(lane16 == 2 * (iota((512, 16), 0) // 128) + py, per_row, 0.0),
+        jnp.where(lane16 == lax.rem(y + 16 - (iota((512, 16), 0) // 128) * sy, NY), per_row, 0.0),
         axis=1,
         keepdims=True,
     )
@@ -550,7 +551,6 @@
     )
 
     recv_all(SPAN_AG, hd, at_h, lambda p: ag.at[p])
-    send_all(ENC_RS, hd, at_h, lambda p: en_send.at[p], en_recv.at[hd])
     sq = jnp.zeros((CAP, 1), F32)
     pieces = []
     for j in range(NHD):
@@ -569,22 +569,20 @@
     def rotate(v):
         return (v * cosine + pltpu.roll(v, HD // 2, 1) * sine).astype(BF16)
 
-    kvbuf[yi, zi, 0] = rotate(column(2))
-    kvbuf[yi, zi, 1] = column(5).astype(BF16)
-    kv_copies = []
-    for dy in range(4):
-        for dz in range(4):
-            if dy + dz > 0:
-                kv_copies.append(
-                    pltpu.make_async_remote_copy(
-                        src_ref=kvbuf.at[yi, zi],
-                        dst_ref=kvbuf.at[yi, zi],
-                        send_sem=kv_sem.at[0, 4 * dy + dz],
-                        recv_sem=kv_sem.at[1, 4 * dy + dz],
-                        device_id=at_class(dy, dz),
-                        device_id_type=MESH,
-                    )
-                )
+    kvbuf[0, 0, 0] = rotate(column(2))
+    kvbuf[0, 0, 1] = column(5).astype(BF16)
+
+    def kv_copy(i, j):
+        return pltpu.make_async_remote_copy(
+            src_ref=kvbuf.at[0, 0],
+            dst_ref=kvbuf.at[i, j],
+            send_sem=kv_sem.at[0, 4 * i + j],
+            recv_sem=kv_sem.at[1, 4 * i + j],
+            device_id=at_slot(i, j),
+            device_id_type=MESH,
+        )
+
+    kv_copies = [kv_copy(i, j) for i, j in SLOTS]
     for copy in kv_copies:
         copy.start()
         pending.append(copy)
@@ -606,24 +604,16 @@
         copy.start()
         pending.append(copy)
 
+    send_all(ENC_RS, hd, at_h, lambda p: en_send.at[p], en_recv.at[hd])
+
     recv_all(ENC_RS, hd, at_h, lambda p: en_recv.at[p])
     encoded = (res.astype(F32) + jnp.sum(en_recv[...].astype(F32), axis=0)).astype(BF16)
 
     for e in range(1, 4):
         slot = qbuf.at[member(e)[1]]
         group_copy(0, e, slot, slot).wait_recv()
-    for dy in range(4):
-        for dz in range(4):
-            if dy + dz > 0:
-                slot = kvbuf.at[lax.rem(yi + 4 - dy, 4), lax.rem(zi + 4 - dz, 4)]
-                pltpu.make_async_remote_copy(
-                    src_ref=slot,
-                    dst_ref=slot,
-                    send_sem=kv_sem.at[0, 4 * dy + dz],
-                    recv_sem=kv_sem.at[1, 4 * dy + dz],
-                    device_id=at_class(dy, dz),
-                    device_id_type=MESH,
-                ).wait_recv()
+    for copy in kv_copies:
+        copy.wait_recv()
 
     kv = kvbuf[...]
     keys = kv[:, :, 0].reshape(512, HD)

time: 74 us -> 69 us (0.932)
  Pallas kernels: 71.1 us -> 66.1 us
    pallas_call x1, Pallas kernels: 71.1 us -> 66.1 us  [shards(): pl.pallas_call(kernel, out_shape=jax.ShapeDtypeStruct((L, 128), BF16), in...]
where the time goes in v4:
time: 69 us; the launch traced here: 68.8 us
  Pallas kernels  66.1 us (96%)
  local copies, waits for them, and re-layouts  1.38 us (2%)
  between operations  1.3 us (2%)
    pallas_call x1, Pallas kernels, shards(): pl.pallas_call(kernel, out_shape=jax.ShapeDtypeStruct((L, 128), BF16), in...  66.1 us

profile of v4, /device:TPU:1, one launch (start us, length us, event | category | flops | bytes accessed | tf_op | source)
XLA Modules:
  0.0 68.8 jit_solution(1544710664232772925)
XLA Ops:
  1.3 66.1 %shard_map.181 = bf16[128,128]{1,0:T(8,128)(2,1)} custom-call(bf16[128,256]{1,0:T(8,128)(2,1)} %x_hbm.1, bf16[128,256]{1,0:T(8,128)(2,1)} %gate_hbm.1, f32[4,256]{1,0:T(4,128)} %convw_ref.1, bf16[128,128]{1,0:T(8,128)(2,1)} %b_hbm.1, bf16[128,128]{1,0:T(8,128)(2,1)} %c_hbm.1, f32[4,128]{1,0:T(4,128)} %bitcast.6, f32[4]{0:T(128)} %decay_ref.1, f32[4]{0:T(128)} %skip_ref.1, ...), custom_call_target="tpu_custom_call" | custom-call | flops 1000000000 | bytes 4000000 | tf_op jit(solution)/shard_map/pallas_call | solution.py:701
  67.4 1.4 %copy.23 = bf16[128,128]{1,0:T(8,128)(2,1)} copy(bf16[128,128]{1,0:T(8,128)(2,1)} %shard_map.181) | data formatting | bytes 65536

commit v5 on v4

--- a/solution.py
+++ b/solution.py
@@ -28,7 +28,7 @@
 SLOTS = sorted(((i, j) for i in range(4) for j in range(4) if i + j > 0), key=lambda t: -t[0] - t[1])
 
 (
-    STATS_Z,
+    EDGE,
     STATS_Y,
     W_AZ,
     W_BY,
@@ -86,24 +86,30 @@
 def kernel(
     x_hbm,
     gate_hbm,
-    convw_ref,
+    convw_hbm,
     b_hbm,
     c_hbm,
+    step_hbm,
+    decay_hbm,
+    skip_hbm,
+    ngain_hbm,
+    mo_hbm,
+    res_hbm,
+    bnd_hbm,
+    pad_hbm,
+    mgain_hbm,
+    wq_hbm,
+    wkv_hbm,
+    mw_hbm,
+    out_ref,
+    convw_ref,
     step_ref,
     decay_ref,
     skip_ref,
     ngain_ref,
-    mo_hbm,
-    res_hbm,
     bnd_ref,
-    cnt_ref,
-    off_ref,
     pad_ref,
     mgain_ref,
-    wq_hbm,
-    wkv_hbm,
-    mw_hbm,
-    out_ref,
     x_ref,
     gate_ref,
     b_ref,
@@ -113,9 +119,8 @@
     wq_ref,
     wkv_ref,
     mw_ref,
-    halo,
     ext,
-    stats_z,
+    ebuf,
     stats_y,
     wbuf,
     s1_send,
@@ -138,7 +143,8 @@
     mn_send,
     mn_recv,
     local_sem,
-    halo_sem,
+    prev_send,
+    prev_recv,
     w0_send,
     w0_recv,
     kv_sem,
@@ -160,9 +166,6 @@
     def at_h(p):
         return (s, p)
 
-    nxt = (lax.rem(s + 1, NY * NZ), hd)
-    prv = (lax.rem(s + NY * NZ - 1, NY * NZ), hd)
-
     py, pz = lax.rem(y, 2), lax.rem(z, 2)
     sy, sz = 1 - 2 * py, 1 - 2 * pz
 
@@ -177,27 +180,36 @@
         return (yc * NZ + zc, hd), 2 * lax.rem(yc, 2) + lax.rem(zc, 2)
 
     barrier = pltpu.get_barrier_semaphore()
-    greet = [prv]
+    greet = [(lax.rem(y + NY - 1, NY) * NZ + NZ - 1, hd)]
     for d in range(1, 8):
         greet += [at_z(lax.rem(z + d, NZ)), at_y(lax.rem(y + d, NY)), at_h(lax.rem(hd + d, NHD))]
     for to in greet:
         pl.semaphore_signal(barrier, inc=1, device_id=to, device_id_type=MESH)
 
     loads = [
+        (step_hbm, step_ref),
+        (decay_hbm, decay_ref),
+        (x_hbm, x_ref),
+        (convw_hbm, convw_ref),
         (b_hbm, b_ref),
-        (c_hbm, c_ref),
-        (x_hbm, x_ref),
         (wq_hbm, wq_ref),
         (wkv_hbm, wkv_ref),
+        (pad_hbm, pad_ref),
+        (mgain_hbm, mgain_ref),
+        (bnd_hbm, bnd_ref),
+        (c_hbm, c_ref),
         (gate_hbm, gate_ref),
+        (skip_hbm, skip_ref),
+        (ngain_hbm, ngain_ref),
+        (res_hbm.at[:, pl.ds(pl.multiple_of(hd * 128, 128), 128)], res_ref),
         (mo_hbm, mo_ref),
-        (res_hbm.at[:, pl.ds(pl.multiple_of(hd * 128, 128), 128)], res_ref),
         (mw_hbm, mw_ref),
     ]
     load = [pltpu.make_async_copy(a, b, local_sem.at[i]) for i, (a, b) in enumerate(loads)]
-    for copy in load:
+    for copy in load[:10]:
         copy.start()
-    l_b, l_c, l_x, l_wq, l_wkv, l_gate, l_mo, l_res, l_mw = load
+    l_step, l_decay, l_x, l_convw, l_b, l_wq, l_wkv, l_pad, l_mgain, l_bnd = load[:10]
+    l_c, l_gate, l_skip, l_ngain, l_res, l_mo, l_mw = load[10:]
 
     pending = []
 
@@ -227,10 +239,13 @@
                 device_id_type=MESH,
             ).wait_recv()
 
+    l_step.wait()
+    l_decay.wait()
+    dec = decay_ref[...]
     row4 = iota((HEADS, L), 0)
     coef = jnp.zeros((HEADS, L), F32)
     for h in range(HEADS):
-        coef = jnp.where(row4 == h, decay_ref[h], coef)
+        coef = jnp.where(row4 == h, dec[:, h : h + 1], coef)
     rate = step_ref[...] * coef
     log_decay = -rate
     gain_row = jnp.sqrt(one_minus_exp(2.0 * rate))
@@ -261,17 +276,89 @@
         [jnp.where(first, run_col[2 * i], run_col[2 * i + 1]) for i in range(2)], axis=1
     )
 
-    pl.semaphore_wait(barrier, len(greet))
-
-    halo_copy = pltpu.make_async_remote_copy(
-        src_ref=x_hbm.at[pl.ds(L - 16, 16), :],
-        dst_ref=halo,
-        send_sem=halo_sem.at[0],
-        recv_sem=halo_sem.at[1],
-        device_id=nxt,
-        device_id_type=MESH,
-    )
-    halo_copy.start()
+    l_x.wait()
+    l_convw.wait()
+    l_b.wait()
+    ext[0:8, :] = jnp.zeros((8, 256), F32)
+    ext[8 : 8 + L, :] = x_ref[...].astype(F32)
+    ext[8 + L :, :] = jnp.zeros((8, 256), F32)
+    cw = convw_ref[...]
+    summed = cw[0:1, :] * ext[5 : 13 + L, :]
+    for k in range(1, 4):
+        summed = summed + cw[k : k + 1, :] * ext[5 + k : 13 + k + L, :]
+    conv_own = silu(summed[:L]).astype(BF16).astype(F32)
+
+    bm = b_ref[...]
+    inner = iota((L, 256), 0) >= 3
+    weighted = jnp.where(inner, conv_own * jnp.concatenate(rem_x, axis=1), 0.0).astype(BF16)
+    state = tn(bm, weighted).astype(BF16)
+    s1_send[...] = state.reshape(8, 16, 256)
+    head_b = bm[0:16, :].astype(F32)
+    ebuf[1 + z, 0:3, 0:256] = summed[0:3]
+    ebuf[1 + z, 3:6, 0:256] = summed[L : L + 3]
+    ebuf[1 + z, 6:7, 0:128] = head_b[0:1, :]
+    ebuf[1 + z, 6:7, 128:256] = head_b[1:2, :]
+    ebuf[1 + z, 7:8, 0:128] = head_b[2:3, :]
+    ebuf[1 + z, 7:8, 128:256] = jnp.zeros((1, 128), F32)
+
+    l_wq.wait()
+    l_wkv.wait()
+    l_pad.wait()
+    l_mgain.wait()
+    l_bnd.wait()
+    prow = s // 2 - 8
+    padf = pad_ref[...].astype(F32)
+    mg = mgain_ref[...]
+    pad_one = jnp.sum(jnp.where(iota((24, 128), 0) == prow, padf, 0.0), axis=0, keepdims=True)
+    gain_one = jnp.sum(jnp.where(iota((32, 128), 0) == s // 2, mg, 0.0), axis=0, keepdims=True)
+    both = pad_one * gain_one
+    half = jnp.where(s % 2 == 1, both[:, 64:], both[:, :64])
+    half = jnp.broadcast_to(half, (16, 64)).astype(BF16)
+    pq = nn(half, wq_ref[...])
+    pkv = nn(half, wkv_ref[...])
+    pad_sq = jnp.sum(jnp.sum(padf * padf, axis=1, keepdims=True), axis=0, keepdims=True)
+    lane1 = iota((1, 128), 1)
+    bounds = bnd_ref[...]
+    count = jnp.sum(jnp.where(bounds < NY * NZ * L, 1.0, 0.0), axis=1, keepdims=True)
+    last = jnp.zeros((1, 128), F32)
+    for h in range(HEADS):
+        last = jnp.where(lane1 == h, run_col[h][L - 1 : L, :], last)
+        for t in range(3):
+            last = jnp.where(lane1 == 16 + 4 * t + h, rem_row[h : h + 1, t : t + 1], last)
+    rows = [
+        pq[0:1, 0:128],
+        pq[0:1, 128:256],
+        pkv[0:1, 0:128],
+        pq[0:1, 256:384],
+        pq[0:1, 384:512],
+        pkv[0:1, 128:256],
+        jnp.where(lane1 == z, count, 0.0),
+        last,
+    ]
+    for i, row in enumerate(rows):
+        ebuf[1 + z, i : i + 1, 256:384] = row
+
+    pl.semaphore_wait(barrier, jnp.where(z == NZ - 1, 21 + NZ, 21))
+
+    send_all(SCAN1, z, at_z, lambda p: s1_send.at[p], s1.at[z])
+    send_all(EDGE, z, at_z, lambda p: ebuf.at[1 + z], ebuf.at[1 + z])
+
+    def prev_copy(p):
+        return pltpu.make_async_remote_copy(
+            src_ref=ebuf.at[1 + z],
+            dst_ref=ebuf.at[0],
+            send_sem=prev_send.at[p],
+            recv_sem=prev_recv.at[0],
+            device_id=(lax.rem(y + 1, NY) * NZ + p, hd),
+            device_id_type=MESH,
+        )
+
+    @pl.when(z == NZ - 1)
+    def _():
+        for p in range(NZ):
+            prev_copy(p).start()
+
+    s1[z] = s1_send[z]
 
     def w0_parts(yp):
         rg = lax.rem(yp, 4)
@@ -312,9 +399,10 @@
         for i, (src, dst) in enumerate(w0_parts(y)):
             pltpu.make_async_copy(src, dst, w0_recv.at[i, y]).start()
 
-    l_b.wait()
+    for copy in load[10:]:
+        copy.start()
+
     l_c.wait()
-    bm = b_ref[...]
     cm = c_ref[...]
     affinity = jnp.where(causal, nt(cm, bm), 0.0)
     mix = []
@@ -322,57 +410,10 @@
         spread = jnp.where(causal, run_col[h] - run_row[h : h + 1, :], 0.0)
         mix.append((jnp.exp(spread) * (affinity * gain_row[h : h + 1, :])).astype(BF16))
 
-    l_wq.wait()
-    l_wkv.wait()
-    prow = s // 2 - 8
-    padf = pad_ref[...].astype(F32)
-    mg = mgain_ref[...]
-    pad_one = jnp.sum(jnp.where(iota((24, 128), 0) == prow, padf, 0.0), axis=0, keepdims=True)
-    gain_one = jnp.sum(jnp.where(iota((32, 128), 0) == s // 2, mg, 0.0), axis=0, keepdims=True)
-    both = pad_one * gain_one
-    half = jnp.where(s % 2 == 1, both[:, 64:], both[:, :64])
-    half = jnp.broadcast_to(half, (16, 64)).astype(BF16)
-    pq = nn(half, wq_ref[...])
-    pkv = nn(half, wkv_ref[...])
-    pad_sq = jnp.sum(jnp.sum(padf * padf, axis=1, keepdims=True), axis=0, keepdims=True)
-    lane1 = iota((1, 128), 1)
-    count = cnt_ref[0].astype(F32)
-    last = jnp.zeros((1, 128), F32)
-    for h in range(HEADS):
-        last = jnp.where(lane1 == h, run_col[h][L - 1 : L, :], last)
-    rows = [
-        pq[0:1, 0:128],
-        pq[0:1, 128:256],
-        pkv[0:1, 0:128],
-        pq[0:1, 256:384],
-        pq[0:1, 384:512],
-        pkv[0:1, 128:256],
-        jnp.where(lane1 == z, count, 0.0),
-        last,
-    ]
-    for i, row in enumerate(rows):
-        stats_z[z, i : i + 1, :] = row
-    send_all(STATS_Z, z, at_z, lambda p: stats_z.at[z], stats_z.at[z])
-
-    l_x.wait()
-    halo_copy.wait()
-    ext[16:, :] = x_ref[...].astype(F32)
-    ext[0:16, :] = jnp.where(s == 0, 0.0, halo[...].astype(F32))
-    cw = convw_ref[...]
-    summed = cw[0:1, :] * ext[13 : 13 + L, :]
-    for k in range(1, 4):
-        summed = summed + cw[k : k + 1, :] * ext[13 + k : 13 + k + L, :]
-    conv = silu(summed).astype(BF16)
-    conv_f = conv.astype(F32)
-
-    weighted = (conv_f * jnp.concatenate(rem_x, axis=1)).astype(BF16)
-    state = tn(bm, weighted).astype(BF16)
-    s1_send[...] = state.reshape(8, 16, 256)
-    send_all(SCAN1, z, at_z, lambda p: s1_send.at[p], s1.at[z])
-    s1[z] = s1_send[z]
-
-    recv_all(STATS_Z, z, at_z, lambda p: stats_z.at[p])
-    tiles = stats_z[...]
+    recv_all(EDGE, z, at_z, lambda p: ebuf.at[1 + p])
+    prev_copy(0).wait_recv()
+    edges = ebuf[...]
+    tiles = edges[1:, :, 256:384]
     stats_y[y] = jnp.sum(tiles, axis=0)
     send_all(STATS_Y, y, at_y, lambda p: stats_y.at[y], stats_y.at[y])
 
@@ -392,6 +433,12 @@
         W_BY, y, at_y, lambda p: wbuf.at[ch_me, 1, z, rg_me], wbuf.at[ch_me, 1, z, rg_me]
     )
 
+    before_rows = pltpu.roll(ebuf[z, :, 0:256], 5, 0)
+    lead = (iota((8, 256), 0) < 3) & (s > 0)
+    top_rows = silu(summed[0:8] + jnp.where(lead, before_rows, 0.0)).astype(BF16).astype(F32)
+    conv_f = jnp.concatenate([top_rows, conv_own[8:]], axis=0)
+    conv = conv_f.astype(BF16)
+
     within = []
     zero = jnp.zeros((), BF16)
     for i in range(2):
@@ -400,18 +447,37 @@
             [jnp.where(first, pair, zero), jnp.where(first, zero, pair)], axis=0
         )
         within.append(nn(jnp.concatenate([mix[2 * i], mix[2 * i + 1]], axis=1), stacked))
+    l_skip.wait()
+    skip_v = skip_ref[...]
     skip = jnp.zeros((1, 256), F32)
     head_of = iota((1, 256), 1) // HP
     for h in range(HEADS):
-        skip = jnp.where(head_of == h, skip_ref[h], skip)
+        skip = jnp.where(head_of == h, skip_v[:, h : h + 1], skip)
     mixed_near = jnp.concatenate(within, axis=1) + skip * conv_f
     exp_run = jnp.exp(run_x)
     l_gate.wait()
     gate = silu(gate_ref[...].astype(F32))
 
-    spread_head = jnp.where(iota((128, 256), 0) == iota((128, 256), 1) // HP, 1.0, 0.0)
-    spread_head = spread_head.astype(F32)
-    lz = nn(tiles[:, 7, :], spread_head, EXACT)
+    col = iota((128, 1024), 1)
+    part_of = col // 256
+    lane_of = lax.rem(col, 256) // HP + jnp.where(part_of > 0, 12 + 4 * part_of, 0)
+    spread_head = jnp.where(iota((128, 1024), 0) == lane_of, 1.0, 0.0).astype(F32)
+    by_head = nn(tiles[:, 7, :], spread_head, EXACT)
+    lz = by_head[:, 0:256]
+
+    nothing = (iota((8, 256), 0) + y) == 0
+    edge_x, edge_b = [], []
+    for t in range(3):
+        earlier = jnp.where(nothing, 0.0, edges[0:8, 3 + t, 0:256])
+        conv_t = silu(edges[1:, t, 0:256] + earlier).astype(BF16).astype(F32)
+        edge_x.append(conv_t * by_head[:, 256 * (1 + t) : 256 * (2 + t)])
+        edge_b.append(edges[1:, 6 + t // 2, 128 * (t % 2) : 128 * (t % 2 + 1)])
+    edge_x = jnp.concatenate(edge_x, axis=0).astype(BF16)
+    edge_b = jnp.concatenate(edge_b, axis=0).astype(BF16)
+    pick_n = jnp.where(si == 16 * z + lax.rem(ti, 16), 1.0, 0.0).astype(BF16)
+    spots = nt(pick_n, edge_b)
+    same = iota((L, 24), 0) // 16 == lax.rem(iota((L, 24), 1), 8)
+    added = nn(jnp.where(same, spots, 0.0).astype(BF16), edge_x).reshape(8, 16, 256)
     recv_all(SCAN1, z, at_z, lambda p: s1.at[p])
     acc = jnp.zeros((16, 256), F32)
     cum = jnp.zeros((1, 256), F32)
@@ -419,7 +485,7 @@
     for j in range(NZ):
         before.append(acc)
         cums.append(cum)
-        acc = jnp.exp(lz[j : j + 1, :]) * acc + s1[j].astype(F32)
+        acc = jnp.exp(lz[j : j + 1, :]) * acc + (s1[j].astype(F32) + added[j])
         cum = cum + lz[j : j + 1, :]
     s2[y] = acc.astype(BF16)
     send_all(SCAN2, y, at_y, lambda p: s2.at[y], s2.at[y])
@@ -464,7 +530,7 @@
     recv_all(STATS_Y, y, at_y, lambda p: stats_y.at[p])
     ytiles = stats_y[...]
     pad_total = jnp.sum(ytiles, axis=0)
-    ly = nn(ytiles[:, 7, :], spread_head, EXACT)
+    ly = nn(ytiles[:, 7, :], spread_head[:, 0:256], EXACT)
 
     recv_all(SCAN2, y, at_y, lambda p: s2.at[p])
     rows_before = jnp.zeros((16, 256), F32)
@@ -479,10 +545,11 @@
     rings(0, True)
     rings(1, False)
 
-    bnd = bnd_ref[...] - s * L
+    l_ngain.wait()
+    bnd = bounds - s * L
     byte_at = iota((L, CAP), 0)
     slot_at = iota((L, CAP), 1)
-    usable = slot_at < cnt_ref[0]
+    usable = bounds < NY * NZ * L
     picker = jnp.where((byte_at == bnd) & usable, 1.0, 0.0).astype(BF16)
     upto = jnp.where((bnd <= byte_at) & usable, 1.0, 0.0)
     newest = jnp.sum(upto, axis=1, keepdims=True) - 1.0
@@ -492,7 +559,12 @@
     res_span = tn(picker, res)
 
     lane = iota((CAP, 128), 1)
-    place = (iota((CAP, 128), 0) + off_ref[0]).astype(F32)
+    counts = ytiles[:, 6, :]
+    lane8 = iota((8, 128), 1)
+    ahead = (lane8 < NZ) & (iota((8, 128), 0) * NZ + lane8 < s)
+    offset = jnp.sum(jnp.where(ahead, counts, 0.0), axis=0, keepdims=True)
+    offset = jnp.sum(offset, axis=1, keepdims=True)
+    place = iota((CAP, 128), 0).astype(F32) + offset
     freq = jnp.exp(
         lax.rem(lane, HD // 2).astype(F32) * (-2.0 * math.log(THETA) / HD)
     )
@@ -605,9 +677,6 @@
         pending.append(copy)
 
     send_all(ENC_RS, hd, at_h, lambda p: en_send.at[p], en_recv.at[hd])
-
-    recv_all(ENC_RS, hd, at_h, lambda p: en_recv.at[p])
-    encoded = (res.astype(F32) + jnp.sum(en_recv[...].astype(F32), axis=0)).astype(BF16)
 
     for e in range(1, 4):
         slot = qbuf.at[member(e)[1]]
@@ -659,6 +728,9 @@
         mn_send[j] = main_part[:, 128 * j : 128 * (j + 1)]
     send_all(MAIN_RS, hd, at_h, lambda p: mn_send.at[p], mn_recv.at[hd])
     mn_recv[hd] = mn_send[hd]
+    recv_all(ENC_RS, hd, at_h, lambda p: en_recv.at[p])
+    encoded = (res.astype(F32) + jnp.sum(en_recv[...].astype(F32), axis=0)).astype(BF16)
+
     recv_all(MAIN_RS, hd, at_h, lambda p: mn_recv.at[p])
     main_rows = (span_share.astype(F32) + jnp.sum(mn_recv[...].astype(F32), axis=0)).astype(BF16)
     out_ref[...] = (encoded.astype(F32) + nn(spreader, main_rows)).astype(BF16)
@@ -670,6 +742,11 @@
     def _():
         for copy in w0_copies():
             copy.wait_send()
+
+    @pl.when(z == NZ - 1)
+    def _():
+        for p in range(NZ):
+            prev_copy(p).wait_send()
 
 
 def shards(
@@ -695,35 +772,22 @@
 ):
     far = pl.BlockSpec(memory_space=pl.ANY)
     near = pl.BlockSpec(memory_space=pltpu.VMEM)
-    scalar = pl.BlockSpec(memory_space=pltpu.SMEM)
     vm = pltpu.VMEM
     dma = pltpu.SemaphoreType.DMA
     return pl.pallas_call(
         kernel,
-        out_shape=jax.ShapeDtypeStruct((L, 128), BF16),
-        in_specs=[
-            far,
-            far,
-            near,
-            far,
-            far,
-            near,
-            scalar,
-            scalar,
-            near,
-            far,
-            far,
-            near,
-            scalar,
-            scalar,
-            near,
-            near,
-            far,
-            far,
-            far,
-        ],
+        out_shape=pltpu.VMEM((L, 128), BF16),
+        in_specs=[far] * 17,
         out_specs=near,
         scratch_shapes=[
+            vm((4, 256), F32),
+            vm((HEADS, L), F32),
+            vm((1, HEADS), F32),
+            vm((1, HEADS), F32),
+            vm((1, 256), F32),
+            vm((1, CAP), jnp.int32),
+            vm((24, 128), BF16),
+            vm((32, 128), F32),
             vm((L, 256), BF16),
             vm((L, 256), BF16),
             vm((L, 128), BF16),
@@ -733,9 +797,8 @@
             vm((64, 512), BF16),
             vm((64, 256), BF16),
             vm((512, 1024), BF16),
-            vm((16, 256), BF16),
             vm((L + 16, 256), F32),
-            vm((8, 8, 128), F32),
+            vm((9, 8, 384), F32),
             vm((8, 8, 128), F32),
             vm((2, 2, 8, 4, 16, 384), BF16),
             vm((8, 16, 256), BF16),
@@ -757,8 +820,9 @@
             vm((4, 8, 128), F32),
             vm((8, CAP, 128), BF16),
             vm((8, CAP, 128), BF16),
-            dma((9,)),
-            dma((2,)),
+            dma((17,)),
+            dma((8,)),
+            dma((1,)),
             dma((2, 8)),
             dma((2, 2)),
             dma((2, 16)),
@@ -777,14 +841,12 @@
         state_write,
         state_read,
         step_size.T,
-        decay_coef,
-        skip_gain,
+        decay_coef.reshape(1, HEADS),
+        skip_gain.reshape(1, HEADS),
         norm_gain.reshape(1, 256),
         mixer_out,
         residual,
         boundaries,
-        span_counts,
-        span_offsets,
         pad_vector.reshape(24, 128),
         main_gain.reshape(32, 128),
         query_weight,

time: 69 us -> 68.4 us (level)
  Pallas kernels: 66.1 us -> 67.6 us
  between operations: 1.3 us -> 0.01 us
  local copies, waits for them, and re-layouts: 1.38 us -> 0.62 us
    pallas_call x1, Pallas kernels: 66.1 us -> 67.6 us  [shards(): pl.pallas_call(kernel, out_shape=pltpu.VMEM((L, 128), BF16), in_specs=[fa...]
    unnamed x1, local copies, waits for them, and re-layouts: 1.38 us -> 0.62 us
where the time goes in v5:
time: 68.4 us; the launch traced here: 68.2 us
  Pallas kernels  67.6 us (99%)
    pallas_call x1, Pallas kernels, shards(): pl.pallas_call(kernel, out_shape=pltpu.VMEM((L, 128), BF16), in_specs=[fa...  67.6 us

profile of v5, /device:TPU:1, one launch (start us, length us, event | category | flops | bytes accessed | tf_op | source)
XLA Modules:
  0.0 68.2 jit_solution(11350912509872606578)
XLA Ops:
  0.0 67.6 %shard_map.163 = bf16[128,128]{1,0:T(8,128)(2,1)S(1)} custom-call(bf16[128,256]{1,0:T(8,128)(2,1)} %x_hbm.1, bf16[128,256]{1,0:T(8,128)(2,1)} %gate_hbm.1, f32[4,256]{1,0:T(4,128)} %convw_hbm.1, bf16[128,128]{1,0:T(8,128)(2,1)} %b_hbm.1, bf16[128,128]{1,0:T(8,128)(2,1)} %c_hbm.1, f32[4,128]{1,0:T(4,128)} %bitcast.8, f32[1,4]{1,0:T(1,128)} %bitcast.10, ...), custom_call_target="tpu_custom_call" | custom-call | flops 1000000000 | bytes 4000000 | tf_op jit(solution)/shard_map/pallas_call | solution.py:777
  67.6 0.6 copy.19

commit v6 on v5

--- a/solution.py
+++ b/solution.py
@@ -166,7 +166,7 @@
     def at_h(p):
         return (s, p)
 
-    py, pz = lax.rem(y, 2), lax.rem(z, 2)
+    py, pz = lax.rem(y + hd, 2), lax.rem(z + hd, 2)
     sy, sz = 1 - 2 * py, 1 - 2 * pz
 
     def at_slot(i, j):
@@ -175,9 +175,9 @@
         return (yc * NZ + zc, hd)
 
     def member(e):
-        yc = y + 1 - 2 * py if e // 2 else y
-        zc = z + 1 - 2 * pz if e % 2 else z
-        return (yc * NZ + zc, hd), 2 * lax.rem(yc, 2) + lax.rem(zc, 2)
+        yc = lax.rem(y + 8 + sy, NY) if e // 2 else y
+        zc = lax.rem(z + 8 + sz, NZ) if e % 2 else z
+        return (yc * NZ + zc, hd), 2 * lax.rem(yc + hd, 2) + lax.rem(zc + hd, 2)
 
     barrier = pltpu.get_barrier_semaphore()
     greet = [(lax.rem(y + NY - 1, NY) * NZ + NZ - 1, hd)]
@@ -340,7 +340,6 @@
 
     pl.semaphore_wait(barrier, jnp.where(z == NZ - 1, 21 + NZ, 21))
 
-    send_all(SCAN1, z, at_z, lambda p: s1_send.at[p], s1.at[z])
     send_all(EDGE, z, at_z, lambda p: ebuf.at[1 + z], ebuf.at[1 + z])
 
     def prev_copy(p):
@@ -358,6 +357,7 @@
         for p in range(NZ):
             prev_copy(p).start()
 
+    send_all(SCAN1, z, at_z, lambda p: s1_send.at[p], s1.at[z])
     s1[z] = s1_send[z]
 
     def w0_parts(yp):
@@ -416,47 +416,6 @@
     tiles = edges[1:, :, 256:384]
     stats_y[y] = jnp.sum(tiles, axis=0)
     send_all(STATS_Y, y, at_y, lambda p: stats_y.at[y], stats_y.at[y])
-
-    for b in range(2):
-        for i, (src, dst) in enumerate(w0_parts(y)):
-            rg = lax.rem(y, 4)
-            ch = y // 4
-            cols = pl.ds(0, 256) if i == 0 else pl.ds(256, 128)
-            slot = wbuf.at[ch, b, z, rg, :, cols]
-            pltpu.make_async_copy(slot, slot, w0_recv.at[i, b]).wait()
-    rg_me = lax.rem(y, 4)
-    ch_me = y // 4
-    send_all(
-        W_AZ, z, at_z, lambda p: wbuf.at[ch_me, 0, z, rg_me], wbuf.at[ch_me, 0, z, rg_me]
-    )
-    send_all(
-        W_BY, y, at_y, lambda p: wbuf.at[ch_me, 1, z, rg_me], wbuf.at[ch_me, 1, z, rg_me]
-    )
-
-    before_rows = pltpu.roll(ebuf[z, :, 0:256], 5, 0)
-    lead = (iota((8, 256), 0) < 3) & (s > 0)
-    top_rows = silu(summed[0:8] + jnp.where(lead, before_rows, 0.0)).astype(BF16).astype(F32)
-    conv_f = jnp.concatenate([top_rows, conv_own[8:]], axis=0)
-    conv = conv_f.astype(BF16)
-
-    within = []
-    zero = jnp.zeros((), BF16)
-    for i in range(2):
-        pair = conv[:, 128 * i : 128 * (i + 1)]
-        stacked = jnp.concatenate(
-            [jnp.where(first, pair, zero), jnp.where(first, zero, pair)], axis=0
-        )
-        within.append(nn(jnp.concatenate([mix[2 * i], mix[2 * i + 1]], axis=1), stacked))
-    l_skip.wait()
-    skip_v = skip_ref[...]
-    skip = jnp.zeros((1, 256), F32)
-    head_of = iota((1, 256), 1) // HP
-    for h in range(HEADS):
-        skip = jnp.where(head_of == h, skip_v[:, h : h + 1], skip)
-    mixed_near = jnp.concatenate(within, axis=1) + skip * conv_f
-    exp_run = jnp.exp(run_x)
-    l_gate.wait()
-    gate = silu(gate_ref[...].astype(F32))
 
     col = iota((128, 1024), 1)
     part_of = col // 256
@@ -489,6 +448,47 @@
         cum = cum + lz[j : j + 1, :]
     s2[y] = acc.astype(BF16)
     send_all(SCAN2, y, at_y, lambda p: s2.at[y], s2.at[y])
+
+    for b in range(2):
+        for i, (src, dst) in enumerate(w0_parts(y)):
+            rg = lax.rem(y, 4)
+            ch = y // 4
+            cols = pl.ds(0, 256) if i == 0 else pl.ds(256, 128)
+            slot = wbuf.at[ch, b, z, rg, :, cols]
+            pltpu.make_async_copy(slot, slot, w0_recv.at[i, b]).wait()
+    rg_me = lax.rem(y, 4)
+    ch_me = y // 4
+    send_all(
+        W_AZ, z, at_z, lambda p: wbuf.at[ch_me, 0, z, rg_me], wbuf.at[ch_me, 0, z, rg_me]
+    )
+    send_all(
+        W_BY, y, at_y, lambda p: wbuf.at[ch_me, 1, z, rg_me], wbuf.at[ch_me, 1, z, rg_me]
+    )
+
+    before_rows = pltpu.roll(ebuf[z, :, 0:256], 5, 0)
+    lead = (iota((8, 256), 0) < 3) & (s > 0)
+    top_rows = silu(summed[0:8] + jnp.where(lead, before_rows, 0.0)).astype(BF16).astype(F32)
+    conv_f = jnp.concatenate([top_rows, conv_own[8:]], axis=0)
+    conv = conv_f.astype(BF16)
+
+    within = []
+    zero = jnp.zeros((), BF16)
+    for i in range(2):
+        pair = conv[:, 128 * i : 128 * (i + 1)]
+        stacked = jnp.concatenate(
+            [jnp.where(first, pair, zero), jnp.where(first, zero, pair)], axis=0
+        )
+        within.append(nn(jnp.concatenate([mix[2 * i], mix[2 * i + 1]], axis=1), stacked))
+    l_skip.wait()
+    skip_v = skip_ref[...]
+    skip = jnp.zeros((1, 256), F32)
+    head_of = iota((1, 256), 1) // HP
+    for h in range(HEADS):
+        skip = jnp.where(head_of == h, skip_v[:, h : h + 1], skip)
+    mixed_near = jnp.concatenate(within, axis=1) + skip * conv_f
+    exp_run = jnp.exp(run_x)
+    l_gate.wait()
+    gate = silu(gate_ref[...].astype(F32))
 
     def block_a(p, lo=0, n=8):
         return wbuf.at[p // 4, 0, pl.ds(lo, n), lax.rem(p, 4)]
@@ -523,10 +523,6 @@
                     copy.start()
                     pending.append(copy)
 
-    recv_all(W_AZ, z, at_z, lambda p: wbuf.at[ch_me, 0, p, rg_me])
-    recv_all(W_BY, y, at_y, lambda p: wbuf.at[p // 4, 1, z, lax.rem(p, 4)])
-    rings(0, False)
-
     recv_all(STATS_Y, y, at_y, lambda p: stats_y.at[p])
     ytiles = stats_y[...]
     pad_total = jnp.sum(ytiles, axis=0)
@@ -541,9 +537,6 @@
         s3_send[j] = (before[j] + jnp.exp(cums[j]) * rows_before).astype(BF16)
     send_all(SCAN3, z, at_z, lambda p: s3_send.at[p], s3.at[z])
     s3[z] = s3_send[z]
-
-    rings(0, True)
-    rings(1, False)
 
     l_ngain.wait()
     bnd = bounds - s * L
@@ -572,6 +565,10 @@
     cosine = jnp.cos(angle)
     sine = jnp.where(lane < HD // 2, -jnp.sin(angle), jnp.sin(angle))
 
+    recv_all(W_AZ, z, at_z, lambda p: wbuf.at[ch_me, 0, p, rg_me])
+    recv_all(W_BY, y, at_y, lambda p: wbuf.at[p // 4, 1, z, lax.rem(p, 4)])
+    rings(0, False)
+
     recv_all(SCAN3, z, at_z, lambda p: s3.at[p])
     entering = nn(cm, s3[...].reshape(128, 256)) * exp_run
     gated = (mixed_near + entering) * gate
@@ -585,13 +582,16 @@
     send_all(SPAN_RS, hd, at_h, lambda p: sp_send.at[p], sp_recv.at[hd])
     sp_recv[hd] = sp_send[hd]
 
-    rings(1, True)
-    rings(2, False)
+    rings(0, True)
+    rings(1, False)
 
     enc_part = nn(normed, mo_ref[...]).astype(BF16)
     for j in range(NHD):
         en_send[j] = enc_part[:, 128 * j : 128 * (j + 1)]
     en_recv[hd] = en_send[hd]
+
+    rings(1, True)
+    rings(2, False)
 
     recv_all(SPAN_RS, hd, at_h, lambda p: sp_recv.at[p])
     span_share = (res_span + jnp.sum(sp_recv[...].astype(F32), axis=0)).astype(BF16)
@@ -618,7 +618,11 @@
     key_ranks[...] = key_rank
     query = iota((1, 512), 1)
     query_rank = (
-        ((y - py + query // 256) * NZ + z - pz + lax.rem(query // 128, 2)) * CAP
+        (
+            lax.rem(y + 8 - py + query // 256, NY) * NZ
+            + lax.rem(z + 8 - pz + lax.rem(query // 128, 2), NZ)
+        )
+        * CAP
         + lax.rem(query, CAP)
     )
 

time: 68.4 us -> 68.3 us (level)
  no operation moved by 1% of the time
where the time goes in v6:
time: 68.3 us; the launch traced here: 68.1 us
  Pallas kernels  67.5 us (99%)
    pallas_call x1, Pallas kernels, shards(): pl.pallas_call(kernel, out_shape=pltpu.VMEM((L, 128), BF16), in_specs=[fa...  67.5 us

profile of v6, /device:TPU:1, one launch (start us, length us, event | category | flops | bytes accessed | tf_op | source)
XLA Modules:
  0.0 68.1 jit_solution(12074569240918491639)
XLA Ops:
  0.0 67.5 %shard_map.163 = bf16[128,128]{1,0:T(8,128)(2,1)S(1)} custom-call(bf16[128,256]{1,0:T(8,128)(2,1)} %x_hbm.1, bf16[128,256]{1,0:T(8,128)(2,1)} %gate_hbm.1, f32[4,256]{1,0:T(4,128)} %convw_hbm.1, bf16[128,128]{1,0:T(8,128)(2,1)} %b_hbm.1, bf16[128,128]{1,0:T(8,128)(2,1)} %c_hbm.1, f32[4,128]{1,0:T(4,128)} %bitcast.8, f32[1,4]{1,0:T(1,128)} %bitcast.10, ...), custom_call_target="tpu_custom_call" | custom-call | flops 1000000000 | bytes 4000000 | tf_op jit(solution)/shard_map/pallas_call | solution.py:781
  67.5 0.6 copy.19

commit v7 on v6

--- a/solution.py
+++ b/solution.py
@@ -32,8 +32,10 @@
     STATS_Y,
     W_AZ,
     W_BY,
-    RING_A,
-    RING_B,
+    RING_A_KV,
+    RING_B_KV,
+    RING_A_Q,
+    RING_B_Q,
     SCAN1,
     SCAN2,
     SCAN3,
@@ -42,7 +44,7 @@
     ENC_RS,
     MAIN_RS,
     N_EX,
-) = range(14)
+) = range(16)
 
 
 def nn(a, b, precision=None):
@@ -340,26 +342,6 @@
 
     pl.semaphore_wait(barrier, jnp.where(z == NZ - 1, 21 + NZ, 21))
 
-    send_all(EDGE, z, at_z, lambda p: ebuf.at[1 + z], ebuf.at[1 + z])
-
-    def prev_copy(p):
-        return pltpu.make_async_remote_copy(
-            src_ref=ebuf.at[1 + z],
-            dst_ref=ebuf.at[0],
-            send_sem=prev_send.at[p],
-            recv_sem=prev_recv.at[0],
-            device_id=(lax.rem(y + 1, NY) * NZ + p, hd),
-            device_id_type=MESH,
-        )
-
-    @pl.when(z == NZ - 1)
-    def _():
-        for p in range(NZ):
-            prev_copy(p).start()
-
-    send_all(SCAN1, z, at_z, lambda p: s1_send.at[p], s1.at[z])
-    s1[z] = s1_send[z]
-
     def w0_parts(yp):
         rg = lax.rem(yp, 4)
         ch = yp // 4
@@ -398,6 +380,26 @@
             copy.start()
         for i, (src, dst) in enumerate(w0_parts(y)):
             pltpu.make_async_copy(src, dst, w0_recv.at[i, y]).start()
+
+    send_all(EDGE, z, at_z, lambda p: ebuf.at[1 + z], ebuf.at[1 + z])
+
+    def prev_copy(p):
+        return pltpu.make_async_remote_copy(
+            src_ref=ebuf.at[1 + z],
+            dst_ref=ebuf.at[0],
+            send_sem=prev_send.at[p],
+            recv_sem=prev_recv.at[0],
+            device_id=(lax.rem(y + 1, NY) * NZ + p, hd),
+            device_id_type=MESH,
+        )
+
+    @pl.when(z == NZ - 1)
+    def _():
+        for p in range(NZ):
+            prev_copy(p).start()
+
+    send_all(SCAN1, z, at_z, lambda p: s1_send.at[p], s1.at[z])
+    s1[z] = s1_send[z]
 
     for copy in load[10:]:
         copy.start()
@@ -490,25 +492,26 @@
     l_gate.wait()
     gate = silu(gate_ref[...].astype(F32))
 
-    def block_a(p, lo=0, n=8):
-        return wbuf.at[p // 4, 0, pl.ds(lo, n), lax.rem(p, 4)]
-
-    def block_b(p, lo=0, n=2):
-        return wbuf.at[pl.ds(lo, n), 1, p]
-
-    def rings(step, wait):
+    def block_a(p, cols, lo=0, n=8):
+        return wbuf.at[p // 4, 0, pl.ds(lo, n), lax.rem(p, 4), :, cols]
+
+    def block_b(p, cols, lo=0, n=2):
+        return wbuf.at[pl.ds(lo, n), 1, p, :, :, cols]
+
+    def rings(step, wait, kv):
+        cols = pl.ds(256, 128) if kv else pl.ds(0, 256)
         for ex, me, where, block, whole in (
-            (RING_A, y, at_y, block_a, 8),
-            (RING_B, z, at_z, block_b, 2),
+            (RING_A_KV if kv else RING_A_Q, y, at_y, block_a, 8),
+            (RING_B_KV if kv else RING_B_Q, z, at_z, block_b, 2),
         ):
             for way in range(2):
                 ahead = lax.rem(me + (1 if way == 0 else 7), 8)
                 moved = step + (1 if wait else 0)
                 of = lax.rem(me + (8 - moved if way == 0 else moved), 8)
                 if step == 3:
-                    part = block(of, way * whole // 2, whole // 2)
+                    part = block(of, cols, way * whole // 2, whole // 2)
                 else:
-                    part = block(of)
+                    part = block(of, cols)
                 copy = pltpu.make_async_remote_copy(
                     src_ref=part,
                     dst_ref=part,
@@ -567,7 +570,8 @@
 
     recv_all(W_AZ, z, at_z, lambda p: wbuf.at[ch_me, 0, p, rg_me])
     recv_all(W_BY, y, at_y, lambda p: wbuf.at[p // 4, 1, z, lax.rem(p, 4)])
-    rings(0, False)
+    rings(0, False, True)
+    rings(0, False, False)
 
     recv_all(SCAN3, z, at_z, lambda p: s3.at[p])
     entering = nn(cm, s3[...].reshape(128, 256)) * exp_run
@@ -582,24 +586,30 @@
     send_all(SPAN_RS, hd, at_h, lambda p: sp_send.at[p], sp_recv.at[hd])
     sp_recv[hd] = sp_send[hd]
 
-    rings(0, True)
-    rings(1, False)
+    rings(0, True, True)
+    rings(1, False, True)
+    rings(0, True, False)
+    rings(1, False, False)
 
     enc_part = nn(normed, mo_ref[...]).astype(BF16)
     for j in range(NHD):
         en_send[j] = enc_part[:, 128 * j : 128 * (j + 1)]
     en_recv[hd] = en_send[hd]
 
-    rings(1, True)
-    rings(2, False)
+    rings(1, True, True)
+    rings(2, False, True)
+    rings(1, True, False)
+    rings(2, False, False)
 
     recv_all(SPAN_RS, hd, at_h, lambda p: sp_recv.at[p])
     span_share = (res_span + jnp.sum(sp_recv[...].astype(F32), axis=0)).astype(BF16)
     ag[hd] = span_share
     send_all(SPAN_AG, hd, at_h, lambda p: ag.at[hd], ag.at[hd])
 
-    rings(2, True)
-    rings(3, False)
+    rings(2, True, True)
+    rings(3, False, True)
+    rings(2, True, False)
+    rings(3, False, False)
 
     key = iota((512, 128), 0)
     key_y = lax.rem(y + 16 - (key // 128) * sy, NY)
@@ -635,18 +645,18 @@
         pieces.append((piece * mg[j : j + 1, :]).astype(BF16))
     scale = lax.rsqrt((sq + pad_sq) * (1.0 / D_MAIN) + EPSILON)
     span_x = jnp.concatenate(pieces, axis=1)
-    rings(3, True)
-    proj = [nn(span_x, wbuf[ch].reshape(1024, 384)) for ch in range(2)]
-
-    def column(i):
-        part = proj[i // 3][:, 128 * (i % 3) : 128 * (i % 3 + 1)]
+    rings(3, True, True)
+    def project(ch, lo, n):
+        return nn(span_x, wbuf[ch, :, :, :, :, lo : lo + n].reshape(1024, n))
+
+    def column(part, i):
         return (part + pad_total[i : i + 1, :]) * scale
 
     def rotate(v):
         return (v * cosine + pltpu.roll(v, HD // 2, 1) * sine).astype(BF16)
 
-    kvbuf[0, 0, 0] = rotate(column(2))
-    kvbuf[0, 0, 1] = column(5).astype(BF16)
+    kvbuf[0, 0, 0] = rotate(column(project(0, 256, 128), 2))
+    kvbuf[0, 0, 1] = column(project(1, 256, 128), 5).astype(BF16)
 
     def kv_copy(i, j):
         return pltpu.make_async_remote_copy(
@@ -663,7 +673,14 @@
         copy.start()
         pending.append(copy)
     mine = 2 * py + pz
-    qbuf[mine] = jnp.concatenate([rotate(column(i)) for i in (0, 1, 3, 4)], axis=0)
+
+    rings(3, True, False)
+    for ch in range(2):
+        pair = project(ch, 0, 256)
+        for h in range(2):
+            at = CAP * (2 * ch + h)
+            part = pair[:, 128 * h : 128 * (h + 1)]
+            qbuf[mine, at : at + CAP, :] = rotate(column(part, 3 * ch + h))
 
     def group_copy(i, e, src, dst):
         return pltpu.make_async_remote_copy(

time: 68.3 us -> 64.4 us (0.943)
  Pallas kernels: 67.5 us -> 63.6 us
    pallas_call x1, Pallas kernels: 67.5 us -> 63.6 us  [shards(): pl.pallas_call(kernel, out_shape=pltpu.VMEM((L, 128), BF16), in_specs=[fa...]
where the time goes in v7:
time: 64.4 us; the launch traced here: 64.3 us
  Pallas kernels  63.6 us (99%)
    pallas_call x1, Pallas kernels, shards(): pl.pallas_call(kernel, out_shape=pltpu.VMEM((L, 128), BF16), in_specs=[fa...  63.6 us

profile of v7, /device:TPU:1, one launch (start us, length us, event | category | flops | bytes accessed | tf_op | source)
XLA Modules:
  0.0 64.3 jit_solution(3803007459140591700)
XLA Ops:
  0.0 63.6 %shard_map.163 = bf16[128,128]{1,0:T(8,128)(2,1)S(1)} custom-call(bf16[128,256]{1,0:T(8,128)(2,1)} %x_hbm.1, bf16[128,256]{1,0:T(8,128)(2,1)} %gate_hbm.1, f32[4,256]{1,0:T(4,128)} %convw_hbm.1, bf16[128,128]{1,0:T(8,128)(2,1)} %b_hbm.1, bf16[128,128]{1,0:T(8,128)(2,1)} %c_hbm.1, f32[4,128]{1,0:T(4,128)} %bitcast.8, f32[1,4]{1,0:T(1,128)} %bitcast.10, ...), custom_call_target="tpu_custom_call" | custom-call | flops 1000000000 | bytes 4000000 | tf_op jit(solution)/shard_map/pallas_call | solution.py:798
  63.6 0.6 copy.19

commit v8 on v7

--- a/solution.py
+++ b/solution.py
@@ -32,10 +32,6 @@
     STATS_Y,
     W_AZ,
     W_BY,
-    RING_A_KV,
-    RING_B_KV,
-    RING_A_Q,
-    RING_B_Q,
     SCAN1,
     SCAN2,
     SCAN3,
@@ -43,8 +39,13 @@
     SPAN_AG,
     ENC_RS,
     MAIN_RS,
+    KV,
+    QUERIES,
+    OUT_SUMS,
+    OUT_STATS,
     N_EX,
 ) = range(16)
+RING_A_KV, RING_B_KV, RING_A_Q, RING_B_Q, N_SEM = (N_EX + 4 * i for i in range(5))
 
 
 def nn(a, b, precision=None):
@@ -145,12 +146,8 @@
     mn_send,
     mn_recv,
     local_sem,
-    prev_send,
-    prev_recv,
-    w0_send,
-    w0_recv,
-    kv_sem,
-    group_sem,
+    prev_sem,
+    w0_sem,
     send_sem,
     recv_sem,
 ):
@@ -214,32 +211,27 @@
     l_c, l_gate, l_skip, l_ngain, l_res, l_mo, l_mw = load[10:]
 
     pending = []
-
-    def send_all(ex, me, where, src, dst):
+    sizes = {}
+
+    def finish(blocks, sem):
+        pltpu.make_async_copy(blocks, blocks, sem).wait()
+
+    def send_all(ex, me, where, src, dst, seven):
         for d in FAR_FIRST:
             p = lax.rem(me + d, 8)
-            copy = pltpu.make_async_remote_copy(
+            pltpu.make_async_remote_copy(
                 src_ref=src(p),
                 dst_ref=dst,
-                send_sem=send_sem.at[ex, d],
-                recv_sem=recv_sem.at[ex, me],
+                send_sem=send_sem.at[ex],
+                recv_sem=recv_sem.at[ex],
                 device_id=where(p),
                 device_id_type=MESH,
-            )
-            copy.start()
-            pending.append(copy)
-
-    def recv_all(ex, me, where, slot):
-        for d in range(1, 8):
-            p = lax.rem(me + 8 - d, 8)
-            pltpu.make_async_remote_copy(
-                src_ref=slot(p),
-                dst_ref=slot(p),
-                send_sem=send_sem.at[ex, d],
-                recv_sem=recv_sem.at[ex, p],
-                device_id=where(p),
-                device_id_type=MESH,
-            ).wait_recv()
+            ).start()
+        pending.append((seven, send_sem.at[ex]))
+        sizes[ex] = seven
+
+    def recv_all(ex):
+        finish(sizes[ex], recv_sem.at[ex])
 
     l_step.wait()
     l_decay.wait()
@@ -366,8 +358,8 @@
                     pltpu.make_async_remote_copy(
                         src_ref=src,
                         dst_ref=dst,
-                        send_sem=w0_send.at[i, d],
-                        recv_sem=w0_recv.at[i, y],
+                        send_sem=w0_sem.at[0, i],
+                        recv_sem=w0_sem.at[1, i],
                         device_id=at_y(yp),
                         device_id_type=MESH,
                     )
@@ -379,16 +371,16 @@
         for copy in w0_copies():
             copy.start()
         for i, (src, dst) in enumerate(w0_parts(y)):
-            pltpu.make_async_copy(src, dst, w0_recv.at[i, y]).start()
-
-    send_all(EDGE, z, at_z, lambda p: ebuf.at[1 + z], ebuf.at[1 + z])
+            pltpu.make_async_copy(src, dst, w0_sem.at[1, i]).start()
+
+    send_all(EDGE, z, at_z, lambda p: ebuf.at[1 + z], ebuf.at[1 + z], ebuf.at[pl.ds(1, 7)])
 
     def prev_copy(p):
         return pltpu.make_async_remote_copy(
             src_ref=ebuf.at[1 + z],
             dst_ref=ebuf.at[0],
-            send_sem=prev_send.at[p],
-            recv_sem=prev_recv.at[0],
+            send_sem=prev_sem.at[0],
+            recv_sem=prev_sem.at[1],
             device_id=(lax.rem(y + 1, NY) * NZ + p, hd),
             device_id_type=MESH,
         )
@@ -398,7 +390,7 @@
         for p in range(NZ):
             prev_copy(p).start()
 
-    send_all(SCAN1, z, at_z, lambda p: s1_send.at[p], s1.at[z])
+    send_all(SCAN1, z, at_z, lambda p: s1_send.at[p], s1.at[z], s1.at[pl.ds(0, 7)])
     s1[z] = s1_send[z]
 
     for copy in load[10:]:
@@ -412,12 +404,12 @@
         spread = jnp.where(causal, run_col[h] - run_row[h : h + 1, :], 0.0)
         mix.append((jnp.exp(spread) * (affinity * gain_row[h : h + 1, :])).astype(BF16))
 
-    recv_all(EDGE, z, at_z, lambda p: ebuf.at[1 + p])
+    recv_all(EDGE)
     prev_copy(0).wait_recv()
     edges = ebuf[...]
     tiles = edges[1:, :, 256:384]
     stats_y[y] = jnp.sum(tiles, axis=0)
-    send_all(STATS_Y, y, at_y, lambda p: stats_y.at[y], stats_y.at[y])
+    send_all(STATS_Y, y, at_y, lambda p: stats_y.at[y], stats_y.at[y], stats_y.at[pl.ds(0, 7)])
 
     col = iota((128, 1024), 1)
     part_of = col // 256
@@ -439,7 +431,7 @@
     spots = nt(pick_n, edge_b)
     same = iota((L, 24), 0) // 16 == lax.rem(iota((L, 24), 1), 8)
     added = nn(jnp.where(same, spots, 0.0).astype(BF16), edge_x).reshape(8, 16, 256)
-    recv_all(SCAN1, z, at_z, lambda p: s1.at[p])
+    recv_all(SCAN1)
     acc = jnp.zeros((16, 256), F32)
     cum = jnp.zeros((1, 256), F32)
     before, cums = [], []
@@ -449,23 +441,17 @@
         acc = jnp.exp(lz[j : j + 1, :]) * acc + (s1[j].astype(F32) + added[j])
         cum = cum + lz[j : j + 1, :]
     s2[y] = acc.astype(BF16)
-    send_all(SCAN2, y, at_y, lambda p: s2.at[y], s2.at[y])
-
-    for b in range(2):
-        for i, (src, dst) in enumerate(w0_parts(y)):
-            rg = lax.rem(y, 4)
-            ch = y // 4
-            cols = pl.ds(0, 256) if i == 0 else pl.ds(256, 128)
-            slot = wbuf.at[ch, b, z, rg, :, cols]
-            pltpu.make_async_copy(slot, slot, w0_recv.at[i, b]).wait()
+    send_all(SCAN2, y, at_y, lambda p: s2.at[y], s2.at[y], s2.at[pl.ds(0, 7)])
+
+    for i, cols in enumerate((pl.ds(0, 256), pl.ds(256, 128))):
+        finish(wbuf.at[0, :, z, 0, :, cols], w0_sem.at[1, i])
     rg_me = lax.rem(y, 4)
     ch_me = y // 4
-    send_all(
-        W_AZ, z, at_z, lambda p: wbuf.at[ch_me, 0, z, rg_me], wbuf.at[ch_me, 0, z, rg_me]
-    )
-    send_all(
-        W_BY, y, at_y, lambda p: wbuf.at[ch_me, 1, z, rg_me], wbuf.at[ch_me, 1, z, rg_me]
-    )
+    pieces7 = wbuf.at[ch_me, 0, pl.ds(0, 7), rg_me]
+    own_a = wbuf.at[ch_me, 0, z, rg_me]
+    own_b = wbuf.at[ch_me, 1, z, rg_me]
+    send_all(W_AZ, z, at_z, lambda p: own_a, own_a, pieces7)
+    send_all(W_BY, y, at_y, lambda p: own_b, own_b, pieces7)
 
     before_rows = pltpu.roll(ebuf[z, :, 0:256], 5, 0)
     lead = (iota((8, 256), 0) < 3) & (s > 0)
@@ -504,41 +490,46 @@
             (RING_A_KV if kv else RING_A_Q, y, at_y, block_a, 8),
             (RING_B_KV if kv else RING_B_Q, z, at_z, block_b, 2),
         ):
+            sems = send_sem.at[ex + step], recv_sem.at[ex + step]
+            if step == 3:
+                moved = block(lax.rem(me + 4, 8), cols)
+            elif block is block_a:
+                moved = wbuf.at[:, 0, :, 0, :, cols]
+            else:
+                moved = wbuf.at[:, 1, pl.ds(0, 2), :, :, cols]
+            if wait:
+                finish(moved, sems[1])
+                continue
             for way in range(2):
                 ahead = lax.rem(me + (1 if way == 0 else 7), 8)
-                moved = step + (1 if wait else 0)
-                of = lax.rem(me + (8 - moved if way == 0 else moved), 8)
+                of = lax.rem(me + (8 - step if way == 0 else step), 8)
                 if step == 3:
                     part = block(of, cols, way * whole // 2, whole // 2)
                 else:
                     part = block(of, cols)
-                copy = pltpu.make_async_remote_copy(
+                pltpu.make_async_remote_copy(
                     src_ref=part,
                     dst_ref=part,
-                    send_sem=send_sem.at[ex, 2 * step + way],
-                    recv_sem=recv_sem.at[ex, 2 * step + way],
+                    send_sem=sems[0],
+                    recv_sem=sems[1],
                     device_id=where(ahead),
                     device_id_type=MESH,
-                )
-                if wait:
-                    copy.wait_recv()
-                else:
-                    copy.start()
-                    pending.append(copy)
-
-    recv_all(STATS_Y, y, at_y, lambda p: stats_y.at[p])
+                ).start()
+            pending.append((moved, sems[0]))
+
+    recv_all(STATS_Y)
     ytiles = stats_y[...]
     pad_total = jnp.sum(ytiles, axis=0)
     ly = nn(ytiles[:, 7, :], spread_head[:, 0:256], EXACT)
 
-    recv_all(SCAN2, y, at_y, lambda p: s2.at[p])
+    recv_all(SCAN2)
     rows_before = jnp.zeros((16, 256), F32)
     for j in range(NY - 1):
         longer = jnp.exp(ly[j : j + 1, :]) * rows_before + s2[j].astype(F32)
         rows_before = jnp.where(j < y, longer, rows_before)
     for j in range(NZ):
         s3_send[j] = (before[j] + jnp.exp(cums[j]) * rows_before).astype(BF16)
-    send_all(SCAN3, z, at_z, lambda p: s3_send.at[p], s3.at[z])
+    send_all(SCAN3, z, at_z, lambda p: s3_send.at[p], s3.at[z], s3.at[pl.ds(0, 7)])
     s3[z] = s3_send[z]
 
     l_ngain.wait()
@@ -568,12 +559,12 @@
     cosine = jnp.cos(angle)
     sine = jnp.where(lane < HD // 2, -jnp.sin(angle), jnp.sin(angle))
 
-    recv_all(W_AZ, z, at_z, lambda p: wbuf.at[ch_me, 0, p, rg_me])
-    recv_all(W_BY, y, at_y, lambda p: wbuf.at[p // 4, 1, z, lax.rem(p, 4)])
+    recv_all(W_AZ)
+    recv_all(W_BY)
     rings(0, False, True)
     rings(0, False, False)
 
-    recv_all(SCAN3, z, at_z, lambda p: s3.at[p])
+    recv_all(SCAN3)
     entering = nn(cm, s3[...].reshape(128, 256)) * exp_run
     gated = (mixed_near + entering) * gate
     mean_sq = jnp.sum(gated * gated, axis=1, keepdims=True) * (1.0 / 256)
@@ -583,7 +574,7 @@
     span_part = nn(picked, mo_ref[...]).astype(BF16)
     for j in range(NHD):
         sp_send[j] = span_part[:, 128 * j : 128 * (j + 1)]
-    send_all(SPAN_RS, hd, at_h, lambda p: sp_send.at[p], sp_recv.at[hd])
+    send_all(SPAN_RS, hd, at_h, lambda p: sp_send.at[p], sp_recv.at[hd], sp_recv.at[pl.ds(0, 7)])
     sp_recv[hd] = sp_send[hd]
 
     rings(0, True, True)
@@ -601,10 +592,10 @@
     rings(1, True, False)
     rings(2, False, False)
 
-    recv_all(SPAN_RS, hd, at_h, lambda p: sp_recv.at[p])
+    recv_all(SPAN_RS)
     span_share = (res_span + jnp.sum(sp_recv[...].astype(F32), axis=0)).astype(BF16)
     ag[hd] = span_share
-    send_all(SPAN_AG, hd, at_h, lambda p: ag.at[hd], ag.at[hd])
+    send_all(SPAN_AG, hd, at_h, lambda p: ag.at[hd], ag.at[hd], ag.at[pl.ds(0, 7)])
 
     rings(2, True, True)
     rings(3, False, True)
@@ -636,13 +627,14 @@
         + lax.rem(query, CAP)
     )
 
-    recv_all(SPAN_AG, hd, at_h, lambda p: ag.at[p])
-    sq = jnp.zeros((CAP, 1), F32)
+    recv_all(SPAN_AG)
+    sq = jnp.zeros((CAP, 128), F32)
     pieces = []
     for j in range(NHD):
         piece = ag[j].astype(F32)
-        sq = sq + jnp.sum(piece * piece, axis=1, keepdims=True)
+        sq = sq + piece * piece
         pieces.append((piece * mg[j : j + 1, :]).astype(BF16))
+    sq = jnp.sum(sq, axis=1, keepdims=True)
     scale = lax.rsqrt((sq + pad_sq) * (1.0 / D_MAIN) + EPSILON)
     span_x = jnp.concatenate(pieces, axis=1)
     rings(3, True, True)
@@ -655,23 +647,22 @@
     def rotate(v):
         return (v * cosine + pltpu.roll(v, HD // 2, 1) * sine).astype(BF16)
 
-    kvbuf[0, 0, 0] = rotate(column(project(0, 256, 128), 2))
-    kvbuf[0, 0, 1] = column(project(1, 256, 128), 5).astype(BF16)
+    kvbuf[0, 0] = rotate(column(project(0, 256, 128), 2))
+    kvbuf[0, 1] = column(project(1, 256, 128), 5).astype(BF16)
 
     def kv_copy(i, j):
         return pltpu.make_async_remote_copy(
-            src_ref=kvbuf.at[0, 0],
-            dst_ref=kvbuf.at[i, j],
-            send_sem=kv_sem.at[0, 4 * i + j],
-            recv_sem=kv_sem.at[1, 4 * i + j],
+            src_ref=kvbuf.at[0],
+            dst_ref=kvbuf.at[4 * i + j],
+            send_sem=send_sem.at[KV],
+            recv_sem=recv_sem.at[KV],
             device_id=at_slot(i, j),
             device_id_type=MESH,
         )
 
-    kv_copies = [kv_copy(i, j) for i, j in SLOTS]
-    for copy in kv_copies:
-        copy.start()
-        pending.append(copy)
+    for i, j in SLOTS:
+        kv_copy(i, j).start()
+    pending.append((kvbuf.at[pl.ds(0, 15)], send_sem.at[KV]))
     mine = 2 * py + pz
 
     rings(3, True, False)
@@ -686,28 +677,24 @@
         return pltpu.make_async_remote_copy(
             src_ref=src,
             dst_ref=dst,
-            send_sem=group_sem.at[0, i, e],
-            recv_sem=group_sem.at[1, i, e],
+            send_sem=send_sem.at[i],
+            recv_sem=recv_sem.at[i],
             device_id=member(e)[0],
             device_id_type=MESH,
         )
 
     for e in range(1, 4):
-        copy = group_copy(0, e, qbuf.at[mine], qbuf.at[mine])
-        copy.start()
-        pending.append(copy)
-
-    send_all(ENC_RS, hd, at_h, lambda p: en_send.at[p], en_recv.at[hd])
-
-    for e in range(1, 4):
-        slot = qbuf.at[member(e)[1]]
-        group_copy(0, e, slot, slot).wait_recv()
-    for copy in kv_copies:
-        copy.wait_recv()
+        group_copy(QUERIES, e, qbuf.at[mine], qbuf.at[mine]).start()
+    pending.append((qbuf.at[pl.ds(0, 3)], send_sem.at[QUERIES]))
+
+    send_all(ENC_RS, hd, at_h, lambda p: en_send.at[p], en_recv.at[hd], en_recv.at[pl.ds(0, 7)])
+
+    finish(qbuf.at[pl.ds(0, 3)], recv_sem.at[QUERIES])
+    finish(kvbuf.at[pl.ds(0, 15)], recv_sem.at[KV])
 
     kv = kvbuf[...]
-    keys = kv[:, :, 0].reshape(512, HD)
-    values = kv[:, :, 1].reshape(512, HD)
+    keys = kv[:, 0].reshape(512, HD)
+    values = kv[:, 1].reshape(512, HD)
     ranks = key_ranks[...]
     unit = 1.0 / math.sqrt(HD)
     for m in range(4):
@@ -722,16 +709,16 @@
 
     for e in range(1, 4):
         place_e = member(e)[1]
-        for i, (src, dst) in enumerate(((o_send, o_recv), (m_send, m_recv))):
-            copy = group_copy(1 + i, e, src.at[place_e], dst.at[e])
-            copy.start()
-            pending.append(copy)
+        group_copy(OUT_SUMS, e, o_send.at[place_e], o_recv.at[e]).start()
+        group_copy(OUT_STATS, e, m_send.at[place_e], m_recv.at[e]).start()
+    sums3, stats3 = o_recv.at[pl.ds(1, 3)], m_recv.at[pl.ds(1, 3)]
+    pending.append((sums3, send_sem.at[OUT_SUMS]))
+    pending.append((stats3, send_sem.at[OUT_STATS]))
     o_recv[0] = o_send[mine]
     m_recv[0] = m_send[mine]
 
-    for e in range(1, 4):
-        group_copy(1, e, o_recv.at[e], o_recv.at[e]).wait_recv()
-        group_copy(2, e, m_recv.at[e], m_recv.at[e]).wait_recv()
+    finish(sums3, recv_sem.at[OUT_SUMS])
+    finish(stats3, recv_sem.at[OUT_STATS])
 
     tops = m_recv[:, 0, :]
     highest = jnp.max(tops, axis=0, keepdims=True)
@@ -747,27 +734,26 @@
     main_part = nn(att, mw_ref[...]).astype(BF16)
     for j in range(NHD):
         mn_send[j] = main_part[:, 128 * j : 128 * (j + 1)]
-    send_all(MAIN_RS, hd, at_h, lambda p: mn_send.at[p], mn_recv.at[hd])
+    send_all(MAIN_RS, hd, at_h, lambda p: mn_send.at[p], mn_recv.at[hd], mn_recv.at[pl.ds(0, 7)])
     mn_recv[hd] = mn_send[hd]
-    recv_all(ENC_RS, hd, at_h, lambda p: en_recv.at[p])
+    recv_all(ENC_RS)
     encoded = (res.astype(F32) + jnp.sum(en_recv[...].astype(F32), axis=0)).astype(BF16)
 
-    recv_all(MAIN_RS, hd, at_h, lambda p: mn_recv.at[p])
+    recv_all(MAIN_RS)
     main_rows = (span_share.astype(F32) + jnp.sum(mn_recv[...].astype(F32), axis=0)).astype(BF16)
     out_ref[...] = (encoded.astype(F32) + nn(spreader, main_rows)).astype(BF16)
 
-    for copy in pending:
-        copy.wait_send()
+    for blocks, sem in pending:
+        finish(blocks, sem)
 
     @pl.when(y < 2)
     def _():
-        for copy in w0_copies():
-            copy.wait_send()
+        for i, cols in enumerate((pl.ds(0, 256), pl.ds(256, 128))):
+            finish(wbuf.at[0, 0, pl.ds(0, 7), 0, :, cols], w0_sem.at[0, i])
 
     @pl.when(z == NZ - 1)
     def _():
-        for p in range(NZ):
-            prev_copy(p).wait_send()
+        finish(ebuf.at[pl.ds(0, NZ)], prev_sem.at[0])
 
 
 def shards(
@@ -832,7 +818,7 @@
             vm((8, CAP, 128), BF16),
             vm((8, L, 128), BF16),
             vm((8, L, 128), BF16),
-            vm((4, 4, 2, CAP, 128), BF16),
+            vm((16, 2, CAP, 128), BF16),
             vm((4, 128, 128), BF16),
             vm((512, 128), jnp.int32),
             vm((4, 128, 128), BF16),
@@ -842,14 +828,10 @@
             vm((8, CAP, 128), BF16),
             vm((8, CAP, 128), BF16),
             dma((17,)),
-            dma((8,)),
-            dma((1,)),
-            dma((2, 8)),
+            dma((2,)),
             dma((2, 2)),
-            dma((2, 16)),
-            dma((2, 3, 4)),
-            dma((N_EX, 8)),
-            dma((N_EX, 8)),
+            dma((N_SEM,)),
+            dma((N_SEM,)),
         ],
         compiler_params=pltpu.CompilerParams(
             collective_id=0, has_side_effects=True, vmem_limit_bytes=56 * 1024 * 1024

time: 64.4 us -> 61.9 us (0.961)
  Pallas kernels: 63.6 us -> 61.1 us
    pallas_call x1, Pallas kernels: 63.6 us -> 61.1 us  [shards(): pl.pallas_call(kernel, out_shape=pltpu.VMEM((L, 128), BF16), in_specs=[fa...]
where the time goes in v8:
time: 61.9 us; the launch traced here: 61.8 us
  Pallas kernels  61.1 us (99%)
  local copies, waits for them, and re-layouts  0.62 us (1%)
    pallas_call x1, Pallas kernels, shards(): pl.pallas_call(kernel, out_shape=pltpu.VMEM((L, 128), BF16), in_specs=[fa...  61.1 us

profile of v8, /device:TPU:1, one launch (start us, length us, event | category | flops | bytes accessed | tf_op | source)
XLA Modules:
  0.0 61.8 jit_solution(1726635354217124474)
XLA Ops:
  0.0 61.1 %shard_map.163 = bf16[128,128]{1,0:T(8,128)(2,1)S(1)} custom-call(bf16[128,256]{1,0:T(8,128)(2,1)} %x_hbm.1, bf16[128,256]{1,0:T(8,128)(2,1)} %gate_hbm.1, f32[4,256]{1,0:T(4,128)} %convw_hbm.1, bf16[128,128]{1,0:T(8,128)(2,1)} %b_hbm.1, bf16[128,128]{1,0:T(8,128)(2,1)} %c_hbm.1, f32[4,128]{1,0:T(4,128)} %bitcast.8, f32[1,4]{1,0:T(1,128)} %bitcast.10, ...), custom_call_target="tpu_custom_call" | custom-call | flops 1000000000 | bytes 4000000 | tf_op jit(solution)/shard_map/pallas_call | solution.py:784
  61.1 0.6 copy.19

commit v9 on v8

--- a/solution.py
+++ b/solution.py
@@ -45,7 +45,7 @@
     OUT_STATS,
     N_EX,
 ) = range(16)
-RING_A_KV, RING_B_KV, RING_A_Q, RING_B_Q, N_SEM = (N_EX + 4 * i for i in range(5))
+RING_KV, RING_Q, N_SEM = (N_EX + 4 * i for i in range(3))
 
 
 def nn(a, b, precision=None):
@@ -486,20 +486,16 @@
 
     def rings(step, wait, kv):
         cols = pl.ds(256, 128) if kv else pl.ds(0, 256)
-        for ex, me, where, block, whole in (
-            (RING_A_KV if kv else RING_A_Q, y, at_y, block_a, 8),
-            (RING_B_KV if kv else RING_B_Q, z, at_z, block_b, 2),
-        ):
-            sems = send_sem.at[ex + step], recv_sem.at[ex + step]
-            if step == 3:
-                moved = block(lax.rem(me + 4, 8), cols)
-            elif block is block_a:
-                moved = wbuf.at[:, 0, :, 0, :, cols]
-            else:
-                moved = wbuf.at[:, 1, pl.ds(0, 2), :, :, cols]
-            if wait:
-                finish(moved, sems[1])
-                continue
+        ex = (RING_KV if kv else RING_Q) + step
+        if step == 3:
+            moved = wbuf.at[:, 0, pl.ds(0, 2), :, :, cols]
+        else:
+            moved = wbuf.at[:, :, pl.ds(0, 2), :, :, cols]
+        if wait:
+            finish(moved, recv_sem.at[ex])
+            return
+        pending.append((moved, send_sem.at[ex]))
+        for me, where, block, whole in ((y, at_y, block_a, 8), (z, at_z, block_b, 2)):
             for way in range(2):
                 ahead = lax.rem(me + (1 if way == 0 else 7), 8)
                 of = lax.rem(me + (8 - step if way == 0 else step), 8)
@@ -510,12 +506,11 @@
                 pltpu.make_async_remote_copy(
                     src_ref=part,
                     dst_ref=part,
-                    send_sem=sems[0],
-                    recv_sem=sems[1],
+                    send_sem=send_sem.at[ex],
+                    recv_sem=recv_sem.at[ex],
                     device_id=where(ahead),
                     device_id_type=MESH,
                 ).start()
-            pending.append((moved, sems[0]))
 
     recv_all(STATS_Y)
     ytiles = stats_y[...]
@@ -531,6 +526,11 @@
         s3_send[j] = (before[j] + jnp.exp(cums[j]) * rows_before).astype(BF16)
     send_all(SCAN3, z, at_z, lambda p: s3_send.at[p], s3.at[z], s3.at[pl.ds(0, 7)])
     s3[z] = s3_send[z]
+
+    recv_all(W_AZ)
+    recv_all(W_BY)
+    rings(0, False, True)
+    rings(0, False, False)
 
     l_ngain.wait()
     bnd = bounds - s * L
@@ -545,6 +545,17 @@
     res = res_ref[...]
     res_span = tn(picker, res)
 
+    span_pick = tn(picker, eye)
+    span_c = nn(span_pick.astype(BF16), cm).astype(BF16)
+    span_near = nn(span_pick, mixed_near, EXACT)
+    span_run = nn(span_pick, exp_run, EXACT)
+    span_gate = nn(span_pick, gate, EXACT)
+
+    def normalize(near, read, run, opening, states):
+        gated = (near + nn(read, states) * run) * opening
+        mean_sq = jnp.sum(gated * gated, axis=1, keepdims=True) * (1.0 / 256)
+        return (gated * lax.rsqrt(mean_sq + EPSILON) * ngain_ref[...]).astype(BF16)
+
     lane = iota((CAP, 128), 1)
     counts = ytiles[:, 6, :]
     lane8 = iota((8, 128), 1)
@@ -559,19 +570,11 @@
     cosine = jnp.cos(angle)
     sine = jnp.where(lane < HD // 2, -jnp.sin(angle), jnp.sin(angle))
 
-    recv_all(W_AZ)
-    recv_all(W_BY)
-    rings(0, False, True)
-    rings(0, False, False)
-
     recv_all(SCAN3)
-    entering = nn(cm, s3[...].reshape(128, 256)) * exp_run
-    gated = (mixed_near + entering) * gate
-    mean_sq = jnp.sum(gated * gated, axis=1, keepdims=True) * (1.0 / 256)
-    normed = (gated * lax.rsqrt(mean_sq + EPSILON) * ngain_ref[...]).astype(BF16)
+    states = s3[...].reshape(128, 256)
     l_mo.wait()
-    picked = tn(picker, normed).astype(BF16)
-    span_part = nn(picked, mo_ref[...]).astype(BF16)
+    span_normed = normalize(span_near, span_c, span_run, span_gate, states)
+    span_part = nn(span_normed, mo_ref[...]).astype(BF16)
     for j in range(NHD):
         sp_send[j] = span_part[:, 128 * j : 128 * (j + 1)]
     send_all(SPAN_RS, hd, at_h, lambda p: sp_send.at[p], sp_recv.at[hd], sp_recv.at[pl.ds(0, 7)])
@@ -582,6 +585,7 @@
     rings(0, True, False)
     rings(1, False, False)
 
+    normed = normalize(mixed_near, cm, exp_run, gate, states)
     enc_part = nn(normed, mo_ref[...]).astype(BF16)
     for j in range(NHD):
         en_send[j] = enc_part[:, 128 * j : 128 * (j + 1)]

time: 61.9 us -> 61.6 us (level)
  no operation moved by 1% of the time
where the time goes in v9:
time: 61.6 us; the launch traced here: 61.5 us
  Pallas kernels  60.8 us (99%)
  local copies, waits for them, and re-layouts  0.62 us (1%)
    pallas_call x1, Pallas kernels, shards(): pl.pallas_call(kernel, out_shape=pltpu.VMEM((L, 128), BF16), in_specs=[fa...  60.8 us

profile of v9, /device:TPU:1, one launch (start us, length us, event | category | flops | bytes accessed | tf_op | source)
XLA Modules:
  0.0 61.5 jit_solution(7353602264410289825)
XLA Ops:
  0.0 60.8 %shard_map.163 = bf16[128,128]{1,0:T(8,128)(2,1)S(1)} custom-call(bf16[128,256]{1,0:T(8,128)(2,1)} %x_hbm.1, bf16[128,256]{1,0:T(8,128)(2,1)} %gate_hbm.1, f32[4,256]{1,0:T(4,128)} %convw_hbm.1, bf16[128,128]{1,0:T(8,128)(2,1)} %b_hbm.1, bf16[128,128]{1,0:T(8,128)(2,1)} %c_hbm.1, f32[4,128]{1,0:T(4,128)} %bitcast.8, f32[1,4]{1,0:T(1,128)} %bitcast.10, ...), custom_call_target="tpu_custom_call" | custom-call | flops 1000000000 | bytes 4000000 | tf_op jit(solution)/shard_map/pallas_call | solution.py:788
  60.8 0.6 %copy.19 = bf16[128,128]{1,0:T(8,128)(2,1)} copy(bf16[128,128]{1,0:T(8,128)(2,1)S(1)} %shard_map.163) | data formatting | bytes 65536

commit v10 on v9

--- a/solution.py
+++ b/solution.py
@@ -334,6 +334,26 @@
 
     pl.semaphore_wait(barrier, jnp.where(z == NZ - 1, 21 + NZ, 21))
 
+    send_all(EDGE, z, at_z, lambda p: ebuf.at[1 + z], ebuf.at[1 + z], ebuf.at[pl.ds(1, 7)])
+
+    def prev_copy(p):
+        return pltpu.make_async_remote_copy(
+            src_ref=ebuf.at[1 + z],
+            dst_ref=ebuf.at[0],
+            send_sem=prev_sem.at[0],
+            recv_sem=prev_sem.at[1],
+            device_id=(lax.rem(y + 1, NY) * NZ + p, hd),
+            device_id_type=MESH,
+        )
+
+    @pl.when(z == NZ - 1)
+    def _():
+        for p in range(NZ):
+            prev_copy(p).start()
+
+    send_all(SCAN1, z, at_z, lambda p: s1_send.at[p], s1.at[z], s1.at[pl.ds(0, 7)])
+    s1[z] = s1_send[z]
+
     def w0_parts(yp):
         rg = lax.rem(yp, 4)
         ch = yp // 4
@@ -373,26 +393,6 @@
         for i, (src, dst) in enumerate(w0_parts(y)):
             pltpu.make_async_copy(src, dst, w0_sem.at[1, i]).start()
 
-    send_all(EDGE, z, at_z, lambda p: ebuf.at[1 + z], ebuf.at[1 + z], ebuf.at[pl.ds(1, 7)])
-
-    def prev_copy(p):
-        return pltpu.make_async_remote_copy(
-            src_ref=ebuf.at[1 + z],
-            dst_ref=ebuf.at[0],
-            send_sem=prev_sem.at[0],
-            recv_sem=prev_sem.at[1],
-            device_id=(lax.rem(y + 1, NY) * NZ + p, hd),
-            device_id_type=MESH,
-        )
-
-    @pl.when(z == NZ - 1)
-    def _():
-        for p in range(NZ):
-            prev_copy(p).start()
-
-    send_all(SCAN1, z, at_z, lambda p: s1_send.at[p], s1.at[z], s1.at[pl.ds(0, 7)])
-    s1[z] = s1_send[z]
-
     for copy in load[10:]:
         copy.start()
 
@@ -404,6 +404,14 @@
         spread = jnp.where(causal, run_col[h] - run_row[h : h + 1, :], 0.0)
         mix.append((jnp.exp(spread) * (affinity * gain_row[h : h + 1, :])).astype(BF16))
 
+    col = iota((128, 1024), 1)
+    part_of = col // 256
+    lane_of = lax.rem(col, 256) // HP + jnp.where(part_of > 0, 12 + 4 * part_of, 0)
+    spread_head = jnp.where(iota((128, 1024), 0) == lane_of, 1.0, 0.0).astype(F32)
+    pick_n = jnp.where(si == 16 * z + lax.rem(ti, 16), 1.0, 0.0).astype(BF16)
+    same = iota((L, 24), 0) // 16 == lax.rem(iota((L, 24), 1), 8)
+    nothing = (iota((8, 256), 0) + y) == 0
+
     recv_all(EDGE)
     prev_copy(0).wait_recv()
     edges = ebuf[...]
@@ -411,14 +419,9 @@
     stats_y[y] = jnp.sum(tiles, axis=0)
     send_all(STATS_Y, y, at_y, lambda p: stats_y.at[y], stats_y.at[y], stats_y.at[pl.ds(0, 7)])
 
-    col = iota((128, 1024), 1)
-    part_of = col // 256
-    lane_of = lax.rem(col, 256) // HP + jnp.where(part_of > 0, 12 + 4 * part_of, 0)
-    spread_head = jnp.where(iota((128, 1024), 0) == lane_of, 1.0, 0.0).astype(F32)
     by_head = nn(tiles[:, 7, :], spread_head, EXACT)
     lz = by_head[:, 0:256]
 
-    nothing = (iota((8, 256), 0) + y) == 0
     edge_x, edge_b = [], []
     for t in range(3):
         earlier = jnp.where(nothing, 0.0, edges[0:8, 3 + t, 0:256])
@@ -427,9 +430,7 @@
         edge_b.append(edges[1:, 6 + t // 2, 128 * (t % 2) : 128 * (t % 2 + 1)])
     edge_x = jnp.concatenate(edge_x, axis=0).astype(BF16)
     edge_b = jnp.concatenate(edge_b, axis=0).astype(BF16)
-    pick_n = jnp.where(si == 16 * z + lax.rem(ti, 16), 1.0, 0.0).astype(BF16)
     spots = nt(pick_n, edge_b)
-    same = iota((L, 24), 0) // 16 == lax.rem(iota((L, 24), 1), 8)
     added = nn(jnp.where(same, spots, 0.0).astype(BF16), edge_x).reshape(8, 16, 256)
     recv_all(SCAN1)
     acc = jnp.zeros((16, 256), F32)
@@ -450,8 +451,8 @@
     pieces7 = wbuf.at[ch_me, 0, pl.ds(0, 7), rg_me]
     own_a = wbuf.at[ch_me, 0, z, rg_me]
     own_b = wbuf.at[ch_me, 1, z, rg_me]
+    send_all(W_BY, y, at_y, lambda p: own_b, own_b, pieces7)
     send_all(W_AZ, z, at_z, lambda p: own_a, own_a, pieces7)
-    send_all(W_BY, y, at_y, lambda p: own_b, own_b, pieces7)
 
     before_rows = pltpu.roll(ebuf[z, :, 0:256], 5, 0)
     lead = (iota((8, 256), 0) < 3) & (s > 0)
@@ -489,6 +490,8 @@
         ex = (RING_KV if kv else RING_Q) + step
         if step == 3:
             moved = wbuf.at[:, 0, pl.ds(0, 2), :, :, cols]
+        elif step == 0:
+            moved = wbuf.at[:, :, pl.ds(0, 4), :, :, cols]
         else:
             moved = wbuf.at[:, :, pl.ds(0, 2), :, :, cols]
         if wait:
@@ -496,8 +499,8 @@
             return
         pending.append((moved, send_sem.at[ex]))
         for me, where, block, whole in ((y, at_y, block_a, 8), (z, at_z, block_b, 2)):
-            for way in range(2):
-                ahead = lax.rem(me + (1 if way == 0 else 7), 8)
+            for way, hops in ((0, 2), (1, 2), (0, 1), (1, 1)) if step == 0 else ((0, 1), (1, 1)):
+                ahead = lax.rem(me + (hops if way == 0 else 8 - hops), 8)
                 of = lax.rem(me + (8 - step if way == 0 else step), 8)
                 if step == 3:
                     part = block(of, cols, way * whole // 2, whole // 2)
@@ -581,20 +584,15 @@
     sp_recv[hd] = sp_send[hd]
 
     rings(0, True, True)
-    rings(1, False, True)
+    rings(2, False, True)
     rings(0, True, False)
-    rings(1, False, False)
+    rings(2, False, False)
 
     normed = normalize(mixed_near, cm, exp_run, gate, states)
     enc_part = nn(normed, mo_ref[...]).astype(BF16)
     for j in range(NHD):
         en_send[j] = enc_part[:, 128 * j : 128 * (j + 1)]
     en_recv[hd] = en_send[hd]
-
-    rings(1, True, True)
-    rings(2, False, True)
-    rings(1, True, False)
-    rings(2, False, False)
 
     recv_all(SPAN_RS)
     span_share = (res_span + jnp.sum(sp_recv[...].astype(F32), axis=0)).astype(BF16)

time: 61.6 us -> 61.4 us (level)
  no operation moved by 1% of the time
where the time goes in v10:
time: 61.4 us; the launch traced here: 61.2 us
  Pallas kernels  60.6 us (99%)
  local copies, waits for them, and re-layouts  0.62 us (1%)
    pallas_call x1, Pallas kernels, shards(): pl.pallas_call(kernel, out_shape=pltpu.VMEM((L, 128), BF16), in_specs=[fa...  60.6 us

profile of v10, /device:TPU:1, one launch (start us, length us, event | category | flops | bytes accessed | tf_op | source)
XLA Modules:
  0.0 61.2 jit_solution(3263417794310931152)
XLA Ops:
  0.0 60.6 %shard_map.163 = bf16[128,128]{1,0:T(8,128)(2,1)S(1)} custom-call(bf16[128,256]{1,0:T(8,128)(2,1)} %x_hbm.1, bf16[128,256]{1,0:T(8,128)(2,1)} %gate_hbm.1, f32[4,256]{1,0:T(4,128)} %convw_hbm.1, bf16[128,128]{1,0:T(8,128)(2,1)} %b_hbm.1, bf16[128,128]{1,0:T(8,128)(2,1)} %c_hbm.1, f32[4,128]{1,0:T(4,128)} %bitcast.8, f32[1,4]{1,0:T(1,128)} %bitcast.10, ...), custom_call_target="tpu_custom_call" | custom-call | flops 1000000000 | bytes 4000000 | tf_op jit(solution)/shard_map/pallas_call | solution.py:786
  60.6 0.6 %copy.19 = bf16[128,128]{1,0:T(8,128)(2,1)} copy(bf16[128,128]{1,0:T(8,128)(2,1)S(1)} %shard_map.163) | data formatting | bytes 65536

commit v11 on v10

--- a/solution.py
+++ b/solution.py
@@ -39,12 +39,13 @@
     SPAN_AG,
     ENC_RS,
     MAIN_RS,
-    KV,
+    KEYS,
+    VALUES,
     QUERIES,
     OUT_SUMS,
     OUT_STATS,
     N_EX,
-) = range(16)
+) = range(17)
 RING_KV, RING_Q, N_SEM = (N_EX + 4 * i for i in range(3))
 
 
@@ -136,7 +137,8 @@
     ag,
     en_send,
     en_recv,
-    kvbuf,
+    kbuf,
+    vbuf,
     qbuf,
     key_ranks,
     o_send,
@@ -594,6 +596,7 @@
         en_send[j] = enc_part[:, 128 * j : 128 * (j + 1)]
     en_recv[hd] = en_send[hd]
 
+
     recv_all(SPAN_RS)
     span_share = (res_span + jnp.sum(sp_recv[...].astype(F32), axis=0)).astype(BF16)
     ag[hd] = span_share
@@ -649,22 +652,22 @@
     def rotate(v):
         return (v * cosine + pltpu.roll(v, HD // 2, 1) * sine).astype(BF16)
 
-    kvbuf[0, 0] = rotate(column(project(0, 256, 128), 2))
-    kvbuf[0, 1] = column(project(1, 256, 128), 5).astype(BF16)
-
-    def kv_copy(i, j):
-        return pltpu.make_async_remote_copy(
-            src_ref=kvbuf.at[0],
-            dst_ref=kvbuf.at[4 * i + j],
-            send_sem=send_sem.at[KV],
-            recv_sem=recv_sem.at[KV],
-            device_id=at_slot(i, j),
-            device_id_type=MESH,
-        )
-
-    for i, j in SLOTS:
-        kv_copy(i, j).start()
-    pending.append((kvbuf.at[pl.ds(0, 15)], send_sem.at[KV]))
+    def slot_sends(ex, buf):
+        for i, j in SLOTS:
+            pltpu.make_async_remote_copy(
+                src_ref=buf.at[0],
+                dst_ref=buf.at[4 * i + j],
+                send_sem=send_sem.at[ex],
+                recv_sem=recv_sem.at[ex],
+                device_id=at_slot(i, j),
+                device_id_type=MESH,
+            ).start()
+        pending.append((buf.at[pl.ds(0, 15)], send_sem.at[ex]))
+
+    kbuf[0] = rotate(column(project(0, 256, 128), 2))
+    slot_sends(KEYS, kbuf)
+    vbuf[0] = column(project(1, 256, 128), 5).astype(BF16)
+    slot_sends(VALUES, vbuf)
     mine = 2 * py + pz
 
     rings(3, True, False)
@@ -692,27 +695,31 @@
     send_all(ENC_RS, hd, at_h, lambda p: en_send.at[p], en_recv.at[hd], en_recv.at[pl.ds(0, 7)])
 
     finish(qbuf.at[pl.ds(0, 3)], recv_sem.at[QUERIES])
-    finish(kvbuf.at[pl.ds(0, 15)], recv_sem.at[KV])
-
-    kv = kvbuf[...]
-    keys = kv[:, 0].reshape(512, HD)
-    values = kv[:, 1].reshape(512, HD)
+    finish(kbuf.at[pl.ds(0, 15)], recv_sem.at[KEYS])
+
+    keys = kbuf[...].reshape(512, HD)
     ranks = key_ranks[...]
     unit = 1.0 / math.sqrt(HD)
+    weights = []
     for m in range(4):
         scores = nt(keys, qbuf[m])
         allowed = ranks <= query_rank[:, 128 * m : 128 * (m + 1)]
         scores = jnp.where(allowed, scores * unit, -1e30)
         top = jnp.max(scores, axis=0, keepdims=True)
-        weights = jnp.exp(scores - top)
-        o_send[m] = tn(values, weights.astype(BF16)).astype(BF16)
+        part = jnp.exp(scores - top)
+        weights.append(part.astype(BF16))
         m_send[m, 0:1, :] = top
-        m_send[m, 1:2, :] = jnp.sum(weights, axis=0, keepdims=True)
-
+        m_send[m, 1:2, :] = jnp.sum(part, axis=0, keepdims=True)
     for e in range(1, 4):
-        place_e = member(e)[1]
-        group_copy(OUT_SUMS, e, o_send.at[place_e], o_recv.at[e]).start()
-        group_copy(OUT_STATS, e, m_send.at[place_e], m_recv.at[e]).start()
+        group_copy(OUT_STATS, e, m_send.at[member(e)[1]], m_recv.at[e]).start()
+
+    finish(vbuf.at[pl.ds(0, 15)], recv_sem.at[VALUES])
+    values = vbuf[...].reshape(512, HD)
+    for m in range(4):
+        o_send[m] = tn(values, weights[m]).astype(BF16)
+
+    for e in range(1, 4):
+        group_copy(OUT_SUMS, e, o_send.at[member(e)[1]], o_recv.at[e]).start()
     sums3, stats3 = o_recv.at[pl.ds(1, 3)], m_recv.at[pl.ds(1, 3)]
     pending.append((sums3, send_sem.at[OUT_SUMS]))
     pending.append((stats3, send_sem.at[OUT_STATS]))
@@ -820,7 +827,8 @@
             vm((8, CAP, 128), BF16),
             vm((8, L, 128), BF16),
             vm((8, L, 128), BF16),
-            vm((16, 2, CAP, 128), BF16),
+            vm((16, CAP, 128), BF16),
+            vm((16, CAP, 128), BF16),
             vm((4, 128, 128), BF16),
             vm((512, 128), jnp.int32),
             vm((4, 128, 128), BF16),

time: 61.4 us -> 61.5 us (level)
  no operation moved by 1% of the time
where the time goes in v11:
time: 61.5 us; the launch traced here: 61.3 us
  Pallas kernels  60.7 us (99%)
  local copies, waits for them, and re-layouts  0.62 us (1%)
    pallas_call x1, Pallas kernels, shards(): pl.pallas_call(kernel, out_shape=pltpu.VMEM((L, 128), BF16), in_specs=[fa...  60.7 us

profile of v11, /device:TPU:1, one launch (start us, length us, event | category | flops | bytes accessed | tf_op | source)
XLA Modules:
  0.0 61.3 jit_solution(4967303014619494737)
XLA Ops:
  0.0 60.7 %shard_map.163 = bf16[128,128]{1,0:T(8,128)(2,1)S(1)} custom-call(bf16[128,256]{1,0:T(8,128)(2,1)} %x_hbm.1, bf16[128,256]{1,0:T(8,128)(2,1)} %gate_hbm.1, f32[4,256]{1,0:T(4,128)} %convw_hbm.1, bf16[128,128]{1,0:T(8,128)(2,1)} %b_hbm.1, bf16[128,128]{1,0:T(8,128)(2,1)} %c_hbm.1, f32[4,128]{1,0:T(4,128)} %bitcast.8, f32[1,4]{1,0:T(1,128)} %bitcast.10, ...), custom_call_target="tpu_custom_call" | custom-call | flops 1000000000 | bytes 4000000 | tf_op jit(solution)/shard_map/pallas_call | solution.py:793
  60.7 0.6 %copy.19 = bf16[128,128]{1,0:T(8,128)(2,1)} copy(bf16[128,128]{1,0:T(8,128)(2,1)S(1)} %shard_map.163) | data formatting | bytes 65536
